TPU v7x, 128 devices: a whole 4x4x4 slice. The times are simulated.
128 devices in a mesh: feed: 4 (over x_hi, core), pts: 32 (over x_lo, z, y).
Axes of the slice: x: 4 (x_hi: 2, x_lo: 2; x = x_hi * 2 + x_lo), y: 4, z: 4, core: 2. Of those that a mesh axis runs over, the one named last changes fastest.
Arguments:
- illumination: bfloat16 [2, 200, 16384], P(None, 'feed', 'pts'), may hold values from -48 to 48
- excitation: bfloat16 [2, 200, 200], P(None, None, 'feed'), may hold values from -1.25 to 1.25
- beam_group: int32 [200], replicated, may hold values from 0 to 7
- positions: float32 [2, 16384], P(None, 'pts'), may hold values from -86 to 86
- params: float32 [2, 16384], P(None, 'pts'), may hold values from 0 to 1
- span_rows: int32 [128], P('pts'), may hold values from 0 to 60
- span_cols: int32 [128], P('pts'), may hold values from 0 to 60
- surface_coef: float32 [4096], replicated, may hold values from -2 to 2
- directions: float32 [2, 8192], replicated, may hold values from -0.05 to 0.05
- cover_blocks: int32 [200, 8], replicated, may hold values from 0 to 63
- cover_count: int32 [200], replicated, may hold values from 1 to 8, 900 in all
Outputs:
- objective: float32 [], replicated
- grad_coef: float32 [4096], replicated
- grad_exc: float32 [2, 200, 200], P(None, None, 'feed')
Inputs may be any that keep to these rules, and one draw needn't show every extreme that they name: `cover_blocks`: slots of a beam past its count are padding; a beam may name a block more than once. `cover_count`: some beam has all 8 slots live.
All inputs are finite; a program needn't handle non-finite values.
Results may differ from a plain program's by a relative error of at most 0.012.
The roundings to bfloat16 on the way count: a program that leaves them out, or rounds other values in their place, can miss the bound.
Values may be sent and summed in bfloat16 or wider, within the bound.
A program may use at most 128 MiB of HBM per device.

v0:
```python
import math

import jax
import jax.numpy as jnp
from jax import lax
from jax.sharding import PartitionSpec as P

GROUP_SIZE = 25
BLOCK = 128
NDB = 64
GRP = 4
CBMAX = 8
NCV = 64
NC = 4096


SHARPNESS = 2.0
TWO_PI = 2.0 * math.pi


def spline_basis(coord):
    one_minus = 1.0 - coord
    t_sq = coord * coord
    t_cube = t_sq * coord
    return jnp.stack(
        [
            one_minus * one_minus * one_minus / 6.0,
            (3.0 * t_cube - 6.0 * t_sq + 4.0) / 6.0,
            (-3.0 * t_cube + 3.0 * t_sq + 3.0 * coord + 1.0) / 6.0,
            t_cube / 6.0,
        ]
    )


def spline_weights(params):
    return (spline_basis(params[0])[:, None, :] * spline_basis(params[1])[None, :, :]).reshape(
        16, params.shape[1]
    )


def spline_index(span_rows, span_cols):
    offsets = (
        jnp.arange(4, dtype=jnp.int32)[:, None] * NCV + jnp.arange(4, dtype=jnp.int32)[None, :]
    ).reshape(16)
    span_base = span_rows * NCV + span_cols
    return jnp.repeat(span_base[None, :] + offsets[:, None], BLOCK, axis=1)


def current_terms(illumination, excitation, member):
    masked = excitation * member[None].astype(excitation.dtype)
    stacked_left = jnp.concatenate(
        [jnp.concatenate([masked[0], -masked[1]], 1), jnp.concatenate([masked[1], masked[0]], 1)], 0
    )
    stacked_right = jnp.concatenate([illumination[0], illumination[1]], 0)
    return jnp.dot(stacked_left, stacked_right, preferred_element_type=jnp.float32)


def kernel(positions, height, dir_block):
    dir_x = dir_block[0]
    dir_y = dir_block[1]
    dir_z = jnp.sqrt(1.0 - dir_x * dir_x - dir_y * dir_y)
    phase_arg = TWO_PI * (
        positions[0][:, None] * dir_x[None, :]
        + positions[1][:, None] * dir_y[None, :]
        + height[:, None] * (1.0 + dir_z)[None, :]
    )
    return (
        jnp.cos(phase_arg).astype(jnp.bfloat16),
        jnp.sin(phase_arg).astype(jnp.bfloat16),
        TWO_PI * (1.0 + dir_z),
    )


def forward_fields(current, positions, height, dir_groups, field_scale):
    beam_count = current.shape[0] // 2

    def forward_group_step(acc_pair, dir_block):
        kern_re, kern_im, phase_rate = kernel(positions, height, dir_block)
        prod_cos = jnp.dot(current, kern_re, preferred_element_type=jnp.float32)
        prod_sin = jnp.dot(current, kern_im, preferred_element_type=jnp.float32)
        fld_re = field_scale * (prod_cos[:beam_count] - prod_sin[beam_count:])
        fld_im = field_scale * (prod_sin[:beam_count] + prod_cos[beam_count:])
        return (acc_pair, (fld_re, fld_im))

    ignored, fields = lax.scan(forward_group_step, jnp.zeros((), jnp.float32), dir_groups)
    return fields


def to_grid(sens, group_idx, beam_idx, sub_idx, beam_count):
    sens_grid = jnp.zeros((NDB // GRP, beam_count, GRP, BLOCK), jnp.float32)
    sens_grid = sens_grid.at[group_idx, beam_idx, sub_idx].add(sens.astype(jnp.float32))
    return sens_grid.astype(jnp.bfloat16).reshape(NDB // GRP, beam_count, GRP * BLOCK)


def backward_terms(positions, height, dir_groups, grid_re, grid_im):
    contract = (((1,), (1,)), ((), ()))
    width_rows = 4 * grid_re.shape[1]
    start = (
        jnp.zeros((width_rows, positions.shape[1]), jnp.float32),
        jnp.zeros((width_rows, positions.shape[1]), jnp.float32),
    )

    def backward_group_step(acc_pair, inputs):
        dir_block, sens_re, sens_im = inputs
        kern_re, kern_im, phase_rate = kernel(positions, height, dir_block)
        rated_re = (phase_rate[None, :] * sens_re.astype(jnp.float32)).astype(jnp.bfloat16)
        rated_im = (phase_rate[None, :] * sens_im.astype(jnp.float32)).astype(jnp.bfloat16)
        stacked_left = jnp.concatenate([sens_re, sens_im, rated_re, rated_im], 0)
        back_cos = lax.dot_general(
            stacked_left, kern_re, contract, preferred_element_type=jnp.float32
        )
        back_sin = lax.dot_general(
            stacked_left, kern_im, contract, preferred_element_type=jnp.float32
        )
        return ((acc_pair[0] + back_cos, acc_pair[1] + back_sin), jnp.zeros((), jnp.float32))

    acc_pair, ignored = lax.scan(backward_group_step, start, (dir_groups, grid_re, grid_im))
    return acc_pair


def excitation_grad(grad_re, grad_im, illumination, member):
    g_re = grad_re.astype(jnp.bfloat16)
    g_im = grad_im.astype(jnp.bfloat16)
    stacked_right = jnp.concatenate([illumination[0], illumination[1]], 1)
    contract = (((1,), (1,)), ((), ()))
    grad_real = lax.dot_general(
        jnp.concatenate([g_re, g_im], 1),
        stacked_right,
        contract,
        preferred_element_type=jnp.float32,
    )
    grad_imag = lax.dot_general(
        jnp.concatenate([g_im, -g_re], 1),
        stacked_right,
        contract,
        preferred_element_type=jnp.float32,
    )
    keep_mask = member.astype(jnp.float32)
    return jnp.stack([grad_real * keep_mask, grad_imag * keep_mask])


def soft_parts(whole_re, whole_im, counts):
    column = jnp.arange(CBMAX * BLOCK, dtype=jnp.int32)
    is_live = column[None, :] // BLOCK < counts[:, None]
    neg_gain = -SHARPNESS * (whole_re * whole_re + whole_im * whole_im)
    return jnp.where(is_live, neg_gain, -1e30)


def local(
    illumination,
    excitation,
    beam_group,
    positions,
    params,
    span_rows,
    span_cols,
    surface_coef,
    directions,
    cover_blocks,
    cover_count,
):
    all_beams = excitation.shape[1]
    feeds_local = excitation.shape[2]
    points_local = illumination.shape[2]
    field_scale = 1.0 / math.sqrt(points_local * lax.axis_size("pts"))
    feed_ids = lax.axis_index("feed") * feeds_local + jnp.arange(feeds_local, dtype=jnp.int32)
    member = feed_ids[None, :] // GROUP_SIZE == beam_group[:, None]
    weights = spline_weights(params)
    coef_index = spline_index(span_rows, span_cols)
    height = jnp.sum(weights * surface_coef[coef_index], axis=0)
    partial_cur = current_terms(illumination, excitation, member)
    current = partial_cur.astype(jnp.bfloat16)
    dir_groups = directions.reshape(2, NDB // GRP, GRP * BLOCK).transpose(1, 0, 2)
    fld_re, fld_im = forward_fields(current, positions, height, dir_groups, field_scale)
    group_idx = cover_blocks // GRP
    sub_idx = cover_blocks % GRP
    beam_idx = jnp.arange(all_beams, dtype=jnp.int32)[:, None]
    flat_re = fld_re.reshape(NDB // GRP, all_beams, GRP, BLOCK)[
        group_idx, beam_idx, sub_idx
    ].reshape(all_beams, CBMAX * BLOCK)
    flat_im = fld_im.reshape(NDB // GRP, all_beams, GRP, BLOCK)[
        group_idx, beam_idx, sub_idx
    ].reshape(all_beams, CBMAX * BLOCK)
    whole_re, whole_im = lax.psum((flat_re, flat_im), ("feed", "pts"))
    masked = soft_parts(whole_re, whole_im, cover_count)
    peak_score = jnp.max(masked)
    expo_terms = jnp.exp(masked - peak_score)
    denom_sum = jnp.sum(expo_terms)
    sens_re = (2.0 * (expo_terms / denom_sum) * whole_re).astype(jnp.bfloat16)
    sens_im = (2.0 * (expo_terms / denom_sum) * whole_im).astype(jnp.bfloat16)
    objective = -(peak_score + jnp.log(denom_sum)) / SHARPNESS
    grid_re = to_grid(
        sens_re.reshape(all_beams, CBMAX, BLOCK), group_idx, beam_idx, sub_idx, all_beams
    )
    grid_im = to_grid(
        sens_im.reshape(all_beams, CBMAX, BLOCK), group_idx, beam_idx, sub_idx, all_beams
    )
    back_cos, back_sin = backward_terms(positions, height, dir_groups, grid_re, grid_im)
    grad_cur_re = field_scale * (back_cos[:all_beams] + back_sin[all_beams : 2 * all_beams])
    grad_cur_im = field_scale * (back_cos[all_beams : 2 * all_beams] - back_sin[:all_beams])
    turn_re = back_cos[3 * all_beams :] - back_sin[2 * all_beams : 3 * all_beams]
    turn_im = -back_cos[2 * all_beams : 3 * all_beams] - back_sin[3 * all_beams :]
    cur_f32 = current.astype(jnp.float32)
    slope_part = field_scale * jnp.sum(
        cur_f32[:all_beams] * turn_re + cur_f32[all_beams:] * turn_im, axis=0
    )
    slope = lax.psum(slope_part, "feed")
    coef_local = jax.ops.segment_sum(
        (weights * slope[None, :]).reshape(-1), coef_index.reshape(-1), num_segments=NC
    )
    grad_coef = lax.psum(coef_local, "pts")
    exc_local = excitation_grad(grad_cur_re, grad_cur_im, illumination, member)
    grad_exc = lax.psum(exc_local, "pts")
    return (objective, grad_coef, grad_exc)


def solution(mesh):
    return jax.shard_map(
        local,
        mesh=mesh,
        in_specs=(
            P(None, "feed", "pts"),
            P(None, None, "feed"),
            P(),
            P(None, "pts"),
            P(None, "pts"),
            P("pts"),
            P("pts"),
            P(),
            P(),
            P(),
            P(),
        ),
        out_specs=(P(), P(), P(None, None, "feed")),
        check_vma=False,
    )
```

profile of v0, /device:TPU:6, one launch (start us, length us, event | category | flops | bytes accessed | tf_op | source)
XLA Modules:
  0.0 1019.5 jit_solution(7838995635314274520)
XLA Ops:
  10.8 45.5 %gather_fusion = f32[8192]{0:T(1024)S(1)} fusion(f32[4096]{0:T(1024)S(1)} %copy-done, s32[8192]{0:T(1024)S(1)} %broadcast_clamp_fusion), kind=kCustom, calls=%fused_computation | custom fusion | bytes 98304 | tf_op jit(solution)/shard_map/gather | solution.py:170
  57.9 160.2 %while.25 = (s32[]{:T(128)}, f32[16,200,512]{2,1,0:T(8,128)}, f32[16,200,512]{2,1,0:T(8,128)}, f32[2,512]{1,0:T(2,128)S(1)}, f32[16,2,512]{2,1,0:T(2,128)}, /*in...) while((s32[]{:T(128)}, f32[16,200,512]{2,1,0:T(8,128)}, ...), condition=%wide.region_2.3_spmd, body=%wide.region_1.2_spmd.sunk | while | flops 423512576 | bytes 4962937 | solution.py:85
  68.7 4.1 convolution_bitcast_fusion.5
  218.1 8.2 reshape.245
  226.6 25.0 %gather_fusion.1 = f32[1600,128]{1,0:T(8,128)S(1)} fusion(f32[16,200,4,128]{3,2,1,0:T(4,128)} %reshape.245, s32[1600]{0:T(1024)S(1)} %reshape.273), kind=kCustom, calls=%fused_computation.1 | custom fusion | bytes 1657600 | tf_op jit(solution)/shard_map/gather | solution.py:178
  252.7 8.2 reshape.247
  260.9 24.8 %gather_fusion.2 = f32[1600,128]{1,0:T(8,128)S(1)} fusion(f32[16,200,4,128]{3,2,1,0:T(4,128)} %reshape.247, s32[1600]{0:T(1024)S(1)} %reshape.273), kind=kCustom, calls=%fused_computation.2 | custom fusion | bytes 1657600 | tf_op jit(solution)/shard_map/gather | solution.py:181
  287.3 150.7 %all-reduce.6.cloned.1.call-done = (f32[200,1024]{1,0:T(8,128)}, f32[200,1024]{1,0:T(8,128)}) async-done(((f32[200,1024]{1,0:T(8,128)}, f32[200,1024]{1,0:T(8,128)}), (f32[200,1024]{1,0:T(8,128)}, f32[200,1024]{1,0:T(8,128)})) %all-reduce.6.cloned.1.call-update) | async-done | bytes 1638416 | tf_op jit(solution)/shard_map/psum | solution.py:184
  444.9 14.7 %scatter_custom_fusion.2 = f32[12800,128]{1,0:T(8,128)} fusion(s32[1600]{0:T(1024)S(1)} %reshape.293, f32[1600,128]{1,0:T(8,128)S(1)} %reshape.301, f32[]{:T(128)} %constant.121.clone.1), kind=kCustom, calls=%fused_computation.71 | custom fusion | flops 204800 | bytes 6553604
  467.7 14.7 %scatter_custom_fusion.1 = f32[12800,128]{1,0:T(8,128)} fusion(s32[1600]{0:T(1024)S(1)} %reshape.293, f32[1600,128]{1,0:T(8,128)S(1)} %reshape.295, f32[]{:T(128)} %constant.121.clone.1), kind=kCustom, calls=%fused_computation.73 | custom fusion | flops 204800 | bytes 6553604
  482.4 11.5 %convert_element_type.83 = bf16[12800,128]{1,0:T(8,128)(2,1)S(1)} convert(f32[12800,128]{1,0:T(8,128)} %scatter_custom_fusion.1) | non-fusion elementwise | flops 1638400 | bytes 9830400 | tf_op jit(solution)/shard_map/convert_element_type | solution.py:92
  497.6 230.7 %while.26 = (s32[]{:T(128)}, f32[800,512]{1,0:T(8,128)}, f32[800,512]{1,0:T(8,128)}, bf16[16,200,512]{2,1,0:T(8,128)(2,1)}, bf16[16,200,512]{2,1,0:T(8,128)(2,1)...) while((s32[]{:T(128)}, f32[800,512]{1,0:T(8,128)}, ...), condition=%wide.region_10.11_spmd.clone, body=%wide.region_9.10_spmd.clone.sunk | while | flops 851340288 | bytes 22579400 | solution.py:117
  499.5 5.5 select_add_fusion.5
  505.0 4.4 select_add_fusion.4
  512.5 7.0 select_add_fusion.5
  519.5 4.4 select_add_fusion.4
  527.0 7.0 select_add_fusion.5
  534.0 4.4 select_add_fusion.4
  541.5 7.0 select_add_fusion.5
  548.5 4.4 select_add_fusion.4
  556.0 7.0 select_add_fusion.5
  563.0 4.4 select_add_fusion.4
  570.6 7.0 select_add_fusion.5
  577.6 4.4 select_add_fusion.4
  585.1 7.0 select_add_fusion.5
  592.1 4.4 select_add_fusion.4
  599.6 7.0 select_add_fusion.5
  606.6 4.4 select_add_fusion.4
  614.1 7.0 select_add_fusion.5
  621.1 4.4 select_add_fusion.4
  628.6 7.0 select_add_fusion.5
  635.6 4.4 select_add_fusion.4
  643.1 7.0 select_add_fusion.5
  650.1 4.4 select_add_fusion.4
  657.7 7.0 select_add_fusion.5
  664.7 4.4 select_add_fusion.4
  672.2 7.0 select_add_fusion.5
  679.2 4.4 select_add_fusion.4
  686.7 7.0 select_add_fusion.5
  693.7 4.4 select_add_fusion.4
  701.2 7.0 select_add_fusion.5
  708.2 4.4 select_add_fusion.4
  715.7 7.0 select_add_fusion.5
  722.7 4.4 select_add_fusion.4
  732.8 8.3 psum.37
  742.5 56.9 %scatter_custom_fusion = f32[4096]{0:T(1024)S(1)} fusion(s32[8192]{0:T(1024)S(1)} %bitcast.106, f32[8192]{0:T(1024)S(1)} %mul.390, f32[]{:T(128)} %constant.121.clone.1), kind=kCustom, calls=%fused_computation.139 | custom fusion | flops 8192 | bytes 16388 | tf_op jit(solution)/shard_map/scatter-add | solution.py:208
  799.4 157.0 %psum.38 = f32[4096]{0:T(1024)} all-reduce(f32[4096]{0:T(1024)S(1)} %scatter_custom_fusion), channel_id=1, replica_groups=mesh['feed'=4,'pts'=32] {'pts'}, use_global_device_ids=true, to_apply=%region_14.15 | all-reduce | flops 4096 | bytes 32768 | tf_op jit(solution)/shard_map/psum | solution.py:211
  956.4 53.4 %all-reduce.4.cloned.1.call-done = f32[2,200,50]{1,2,0:T(8,128)} async-done(((f32[2,200,50]{1,2,0:T(8,128)}), f32[2,200,50]{1,2,0:T(8,128)}) %all-reduce.4.cloned.1.call-update) | async-done | bytes 80016 | tf_op jit(solution)/shard_map/psum | solution.py:213
  (311 shorter events, 237.6 us)
Async XLA Ops:
  7.2 3.7 copy-start
  7.2 430.9 %all-reduce.6.cloned.1.call-start = ((), (), s32[]{:S(2)}) async-start(), calls=%async_computation.1 | async-start | bytes 3276800 | tf_op jit(solution)/shard_map/psum | solution.py:184
  10.8 45.6 %copy-start.7 = (bf16[2,50,512]{2,0,1:T(2,128)(2,1)S(1)}, bf16[2,50,512]{2,0,1:T(2,128)(2,1)}, u32[]{:S(2)}) copy-start(bf16[2,50,512]{2,0,1:T(2,128)(2,1)} %param.15) | copy-start | bytes 307204
  56.4 1.5 copy-start.8
  218.1 8.2 copy-start.9
  285.7 1.2 copy-start.12
  285.7 1.3 copy-start.13
  285.7 152.4 %copy-start.10 = (s32[200]{0:T(256)S(1)}, s32[200]{0:T(256)}, u32[]{:S(2)}) copy-start(s32[200]{0:T(256)} %param.25) | copy-start | bytes 2404
  286.8 723.0 %all-reduce.4.cloned.1.call-start = ((), (), s32[]{:S(2)}) async-start(), calls=%async_computation | async-start | bytes 229376 | tf_op jit(solution)/shard_map/psum | solution.py:213
  438.0 2.4 copy-start.2
  438.0 2.4 copy-start.3
  499.5 5.5 copy-start.5
  509.4 1.2 copy-start.6
  512.5 7.0 copy-start.5
  523.9 1.2 copy-start.6
  527.0 7.0 copy-start.5
  538.4 1.2 copy-start.6
  541.5 7.0 copy-start.5
  552.9 1.2 copy-start.6
  556.0 7.0 copy-start.5
  567.4 1.2 copy-start.6
  570.5 7.0 copy-start.5
  582.0 1.2 copy-start.6
  585.1 7.0 copy-start.5
  596.5 1.2 copy-start.6
  599.6 7.0 copy-start.5
  611.0 1.2 copy-start.6
  614.1 7.0 copy-start.5
  625.5 1.2 copy-start.6
  628.6 7.0 copy-start.5
  640.0 1.2 copy-start.6
  643.1 7.0 copy-start.5
  654.6 1.2 copy-start.6
  657.6 7.0 copy-start.5
  669.1 1.2 copy-start.6
  672.2 7.0 copy-start.5
  683.6 1.2 copy-start.6
  686.7 7.0 copy-start.5
  698.1 1.2 copy-start.6
  701.2 7.0 copy-start.5
  712.6 1.2 copy-start.6
  715.7 7.0 copy-start.5
  727.1 1.2 copy-start.6
  728.3 1.4 copy-start.4
  729.7 1.9 copy-start.11
  729.7 281.6 %copy-start.1 = (f32[4096]{0:T(1024)S(1)}, f32[4096]{0:T(1024)}, u32[]{:S(2)}) copy-start(f32[4096]{0:T(1024)} %param.22) | copy-start | bytes 49156
Sparse Core Ops, SparseCore 0:
  286.9 151.0 all-reduce.5
  733.0 276.7 all-reduce.3
where the time goes:
time: 1030 us; the launch traced here: 1020 us
  matrix products  313 us (30%)
  waiting for transfers between devices  204 us (20%)
  local copies, waits for them, and re-layouts  169 us (16%)
  blocking collectives  165 us (16%)
  other arithmetic  151 us (15%)
  between operations  17.1 us (2%)
    psum x1, blocking collectives, local(): grad_coef = lax.psum(coef_local, 'pts')  157 us
    psum x1, waiting for transfers between devices, local(): whole_re, whole_im = lax.psum((flat_re, flat_im), ('feed', 'pts'))  151 us
    dot_general x16, matrix products, backward_group_step(): lax.dot_general(stacked_left, kern_im, contract, preferred_element_type=j...  110 us
    dot_general x16, matrix products, backward_group_step(): lax.dot_general(stacked_left, kern_re, contract, preferred_element_type=j...  70.4 us
    dot_general x16, matrix products, forward_group_step(): prod_sin = jnp.dot(current, kern_im, preferred_element_type=jnp.float32)  65.4 us
    dot_general x16, matrix products, forward_group_step(): prod_cos = jnp.dot(current, kern_re, preferred_element_type=jnp.float32)  64.7 us
    scatter-add x1, other arithmetic, local(): jax.ops.segment_sum((weights * slope[None, :]).reshape(-1), coef_index.re...  56.9 us
    psum x1, waiting for transfers between devices, local(): grad_exc = lax.psum(exc_local, 'pts')  53.4 us
  transfers between devices with their start and end apart: 2, of which 2 were waited for; matrix products, arithmetic and copies ran while one was open for 6% of the time, Pallas kernels for 0%

commit v1 on v0

v1 whole, which is shorter than its diff:
```python
import functools
import math

import jax
import jax.numpy as jnp
from jax import lax
from jax.experimental import pallas as pl
from jax.experimental.pallas import tpu as pltpu
from jax.sharding import PartitionSpec as P

MESH = pl.DeviceIdType.MESH
F32 = jnp.float32
BF16 = jnp.bfloat16

GROUP_SIZE = 25
BEAMS = 200
NDB = 64
BLOCK = 128
CBMAX = 8
NCV = 64
NC = 4096
SHARPNESS = 2.0
TWO_PI = 2.0 * math.pi

FEED = 4
PTSD = 32
PLOC = 512
BP = 256
EB = 208
SLOTS = NDB // FEED
CAP = 384
CH = 24
NEG = -1e30

COS_C = (0.99999921, -19.73898036, 64.92865742, -85.27162153, 58.79049212, -21.07110563)
SIN_C = (6.28318492, -41.34158923, 81.59994333, -76.61447253, 41.34288235, -12.47124354)


def horner(coefs, z):
    acc = jnp.full(z.shape, coefs[-1], F32)
    for c in coefs[-2::-1]:
        acc = acc * z + c
    return acc


def iota(shape, dim):
    return lax.broadcasted_iota(jnp.int32, shape, dim)


def columns(row, n):
    return jnp.transpose(jnp.broadcast_to(row, (n, row.shape[1])))


def dot(a, b):
    return jnp.dot(a, b, preferred_element_type=F32)


def body(
    il_ref, ex_ref, bg_ref, pos_ref, par_ref, row_ref, col_ref, coef_ref, dir_ref, cb_ref, cnt_ref,
    obj_ref, gcoef_ref, gexc_ref,
    il_all, e_all, dirx, diry, xb, yb, hb, w16, kall, rates, pad_a, pad_b,
    rt_s, mt_s, rank_s, rs_s, ms_s, off_s, end_s, ohm, oh, multb, jre, jim, jtre, jtim, jsel,
    fbuf, frecv, agbuf, covre, covim, st, rhs, accs, stats, gbuf, grecv, fb, gag,
    il_ss, il_rs, e_ss, e_rs, rs_ss, rs_rs, ag_ss, ag_rs, st_ss, st_rs, g_ss, g_rs, b_ss, b_rs, c_ss, c_rs,
):
    f = lax.axis_index("feed")
    p = lax.axis_index("pts")
    sib = f + 1 - 2 * (f % 2)
    par = (f + 2) % FEED
    par_sib = (sib + 2) % FEED

    barrier = pltpu.get_barrier_semaphore()

    def greet(d, carry):
        pl.semaphore_signal(barrier, inc=1, device_id={"pts": (p + d) % PTSD}, device_id_type=MESH)
        return carry

    lax.fori_loop(1, PTSD, greet, 0)
    for d in range(1, FEED):
        pl.semaphore_signal(barrier, inc=1, device_id={"feed": (f + d) % FEED}, device_id_type=MESH)

    r64 = iota((64, 50), 0)
    place = jnp.where(
        (iota((64, 50), 1) == GROUP_SIZE * (r64 // 32) + r64 % 32) & (r64 % 32 < GROUP_SIZE), 1.0, 0.0
    ).astype(BF16)
    il_all[f, 0:64, :] = dot(place, il_ref[0]).astype(BF16)
    il_all[f, 64:128, :] = dot(place, il_ref[1]).astype(BF16)

    pad_a[...] = jnp.full((8, BP), -1.0, F32)
    pad_a[0:1, 0:BEAMS] = bg_ref[...].astype(F32)
    grp_row = pad_a[0:1, :]
    l128 = iota((50, 128), 1)
    r50 = iota((50, 128), 0)
    lane_feed = GROUP_SIZE * ((l128 % 64) // 32) + l128 % 32
    fits = (r50 == lane_feed) & (l128 % 32 < GROUP_SIZE)
    q_re = jnp.where(fits & (l128 < 64), 1.0, 0.0).astype(BF16)
    q_im = jnp.where(fits & (l128 >= 64), 1.0, 0.0).astype(BF16)
    ex = dot(ex_ref[0], q_re) + dot(ex_ref[1], q_im)
    grp_cols = columns(grp_row, 128)[0:BEAMS, :]
    lane_grp = ((iota((BEAMS, 128), 1) % 64) // 32 + 2 * f).astype(F32)
    e_all[f, 0:BEAMS, :] = jnp.where(grp_cols == lane_grp, ex, 0.0).astype(BF16)
    e_all[f, BEAMS:EB, :] = jnp.zeros((EB - BEAMS, 128), BF16)

    pl.semaphore_wait(barrier, PTSD - 1 + FEED - 1)

    def feed_copy(buf, slot, target, ss, rs, k):
        return pltpu.make_async_remote_copy(
            src_ref=buf.at[slot], dst_ref=buf.at[slot], send_sem=ss.at[k], recv_sem=rs.at[k],
            device_id={"feed": target}, device_id_type=MESH,
        )

    il_copies = [feed_copy(il_all, f, par, il_ss, il_rs, 0), feed_copy(il_all, f, sib, il_ss, il_rs, 1)]
    e_copies = [feed_copy(e_all, f, par, e_ss, e_rs, 0), feed_copy(e_all, f, sib, e_ss, e_rs, 1)]
    e_copies[0].start()
    il_copies[0].start()
    e_copies[1].start()
    il_copies[1].start()

    pad_b[...] = jnp.full((BP, 128), -1.0, F32)
    pad_b[0:BEAMS, 0:CBMAX] = cb_ref[...].astype(F32)
    pad_a[...] = jnp.zeros((8, BP), F32)
    pad_a[0:1, 0:BEAMS] = cnt_ref[...].astype(F32)
    cover = jnp.transpose(pad_b[...])
    count = pad_a[0:1, :]
    k_io = iota((NDB, BP), 0).astype(F32)
    mult = jnp.zeros((NDB, BP), F32)
    for c in range(CBMAX):
        mult = mult + jnp.where((cover[c : c + 1, :] == k_io) & (count > c), 1.0, 0.0)
    ind = jnp.where(mult > 0.0, 1.0, 0.0)
    n_col = jnp.sum(ind, axis=1, keepdims=True)
    n_b = jnp.broadcast_to(n_col, (NDB, 128))
    n_row = jnp.transpose(jnp.concatenate([n_b, jnp.full((NDB, 128), -1.0, F32)], 0))[0:1, :]
    lane = iota((NDB, 128), 1)
    sub = iota((NDB, 128), 0)
    ahead = (n_row > n_b) | ((n_row == n_b) & (lane < sub))
    rank = jnp.sum(jnp.where(ahead, 1.0, 0.0), axis=1, keepdims=True)
    rank_b = jnp.broadcast_to(rank, (NDB, 128))

    def deal(r):
        level = jnp.floor(r * 0.25)
        odd = level - 2.0 * jnp.floor(level * 0.5)
        place_in = r - 4.0 * level
        return level, jnp.where(odd > 0.5, 3.0 - place_in, place_in)

    fq = f.astype(F32)
    lev_b, bin_b = deal(rank_b)
    rank_row = jnp.transpose(jnp.concatenate([rank_b, jnp.full((NDB, 128), 400.0, F32)], 0))[0:1, :]
    lev_row, bin_row = deal(rank_row)
    before = (bin_row == fq) & (lev_row < lev_b) & (lane < NDB)
    off_col = jnp.sum(jnp.where(before, n_row, 0.0), axis=1, keepdims=True)
    upper = jnp.where(iota((BP, BP), 0) < iota((BP, BP), 1), 1.0, 0.0).astype(BF16)
    prefix = dot(ind.astype(BF16), upper)
    mine = (ind > 0.0) & (bin_b[:, 0:1] == fq)
    rt_s[...] = jnp.where(mine, prefix + off_col, -1.0)
    mt_s[...] = mult
    rank_s[...] = rank_b
    off_b = jnp.broadcast_to(off_col, (NDB, 128))

    def target(s):
        return 4 * s + f + (s % 2) * (3 - 2 * f)

    for s in range(SLOTS):
        is_s = rank_b == target(s).astype(F32)
        off = jnp.sum(jnp.where(is_s, off_b, 0.0), axis=0, keepdims=True)
        off_s[s : s + 1, :] = off
        end_s[s : s + 1, :] = off + jnp.sum(jnp.where(is_s, n_b, 0.0), axis=0, keepdims=True)
        is_w = is_s[:, 0:1]
        rs_s[s : s + 1, :] = jnp.sum(jnp.where(is_w, rt_s[...], 0.0), axis=0, keepdims=True)
        ms_s[s : s + 1, :] = jnp.sum(jnp.where(is_w, mt_s[...], 0.0), axis=0, keepdims=True)

    def one_hot(rc, carry):
        base = pl.multiple_of(rc * 128, 128)
        rows = (iota((128, BP), 0) + base).astype(F32)
        acc = jnp.zeros((128, BP), F32)
        for s in range(SLOTS):
            acc = jnp.where(rs_s[s : s + 1, :] == rows, ms_s[s : s + 1, :], acc)
        ohm[pl.ds(base, 128), :] = acc.astype(BF16)
        oh[pl.ds(base, 128), :] = jnp.where(acc > 0.0, 1.0, 0.0).astype(BF16)
        multb[pl.ds(base, 128), :] = jnp.broadcast_to(jnp.sum(acc, axis=1, keepdims=True), (128, 128))
        return carry

    lax.fori_loop(0, CAP // 128, one_hot, 0)

    def basis(t):
        m = 1.0 - t
        t2 = t * t
        t3 = t2 * t
        return [
            m * m * m / 6.0,
            (3.0 * t3 - 6.0 * t2 + 4.0) / 6.0,
            (-3.0 * t3 + 3.0 * t2 + 3.0 * t + 1.0) / 6.0,
            t3 / 6.0,
        ]

    bu = basis(par_ref[0:1, :])
    bv = basis(par_ref[1:2, :])
    for i in range(4):
        for j in range(4):
            w16[4 * i + j : 4 * i + j + 1, :] = bu[i] * bv[j]
    heights = []
    for blk in range(PLOC // BLOCK):
        base = row_ref[blk] * NCV + col_ref[blk]
        h = jnp.zeros((1, BLOCK), F32)
        for i in range(4):
            for j in range(4):
                k = 4 * i + j
                h = h + w16[k : k + 1, blk * BLOCK : (blk + 1) * BLOCK] * coef_ref[base + i * NCV + j]
        heights.append(h)
    hb[...] = columns(jnp.concatenate(heights, axis=1), 128)
    xb[...] = columns(pos_ref[0:1, :], 128)
    yb[...] = columns(pos_ref[1:2, :], 128)

    for k in range(NDB):
        dirx[k : k + 1, :] = dir_ref[0:1, k * BLOCK : (k + 1) * BLOCK]
        diry[k : k + 1, :] = dir_ref[1:2, k * BLOCK : (k + 1) * BLOCK]

    def phases(s, carry):
        is_s = rank_s[...] == target(s).astype(F32)
        ux = jnp.sum(jnp.where(is_s, dirx[...], 0.0), axis=0, keepdims=True)
        uy = jnp.sum(jnp.where(is_s, diry[...], 0.0), axis=0, keepdims=True)
        uz1 = 1.0 + jnp.sqrt(1.0 - ux * ux - uy * uy)
        rates[s] = columns(TWO_PI * uz1, 128)
        base = pl.multiple_of(s * 256, 256)
        for c in range(PLOC // 64):
            rows = pl.ds(64 * c, 64)
            t = xb[rows, :] * ux + yb[rows, :] * uy + hb[rows, :] * uz1
            r = t - jnp.round(t)
            z = r * r
            kall[rows, pl.ds(base, 128)] = horner(COS_C, z).astype(BF16)
            kall[rows, pl.ds(base + 128, 128)] = (r * horner(SIN_C, z)).astype(BF16)
        return carry

    lax.fori_loop(0, SLOTS, phases, 0)

    e_copies[0].wait_recv()
    e_copies.append(feed_copy(e_all, par, sib, e_ss, e_rs, 2))
    e_copies[2].start()
    il_copies[0].wait_recv()
    il_copies.append(feed_copy(il_all, par, sib, il_ss, il_rs, 2))
    il_copies[2].start()
    for k in (1, 2):
        e_copies[k].wait_recv()
        il_copies[k].wait_recv()

    exc = jnp.concatenate([e_all[k] for k in range(FEED)], axis=1)
    left = [il_all[k] for k in range(FEED)]
    mix_re = jnp.concatenate([x for b in left for x in (b[0:64, :], -b[64:128, :])], axis=0)
    mix_im = jnp.concatenate([x for b in left for x in (b[64:128, :], b[0:64, :])], axis=0)
    jre[EB:BP, :] = jnp.zeros((BP - EB, PLOC), BF16)
    jim[EB:BP, :] = jnp.zeros((BP - EB, PLOC), BF16)
    jre[0:EB, :] = dot(exc, mix_re).astype(BF16)
    jim[0:EB, :] = dot(exc, mix_im).astype(BF16)
    jsel[0:CAP, :] = dot(oh[...], jre[...]).astype(BF16)
    jsel[CAP : 2 * CAP, :] = dot(oh[...], jim[...]).astype(BF16)

    covre[...] = jnp.zeros((CAP, BLOCK), F32)
    covim[...] = jnp.zeros((CAP, BLOCK), F32)
    scale = 1.0 / math.sqrt(PLOC * PTSD)

    def forward(s, carry):
        base = pl.multiple_of(s * 256, 256)
        prod = dot(jsel[...], kall[:, pl.ds(base, 256)])
        row = iota((CAP, BLOCK), 0).astype(F32)
        own = (row >= off_s[pl.ds(s, 1), :]) & (row < end_s[pl.ds(s, 1), :])
        re = prod[0:CAP, 0:128] - prod[CAP:, 128:]
        im = prod[0:CAP, 128:] + prod[CAP:, 0:128]
        covre[...] = jnp.where(own, re, covre[...])
        covim[...] = jnp.where(own, im, covim[...])
        return carry

    lax.fori_loop(0, SLOTS, forward, 0)

    low = iota((8, BLOCK), 0) < 4
    for c in range(PTSD):
        fbuf[c, 0:8, :] = scale * covre[8 * c : 8 * c + 8, :]
        fbuf[c, 8:16, :] = scale * covim[8 * c : 8 * c + 8, :]
    for t in range(PTSD // 2):
        re = scale * covre[256 + 8 * t : 264 + 8 * t, :]
        im = scale * covim[256 + 8 * t : 264 + 8 * t, :]
        fbuf[2 * t, 16:24, :] = jnp.where(low, re, pltpu.roll(im, 4, 0))
        fbuf[2 * t + 1, 16:24, :] = jnp.where(low, pltpu.roll(re, 4, 0), im)

    def scatter_copy(d, src, dst, ss, rs):
        to = (p + d) % PTSD
        return pltpu.make_async_remote_copy(
            src_ref=src.at[to], dst_ref=dst.at[d - 1], send_sem=ss, recv_sem=rs,
            device_id={"pts": to}, device_id_type=MESH,
        )

    def gather_copy(d, buf, ss, rs):
        return pltpu.make_async_remote_copy(
            src_ref=buf.at[p], dst_ref=buf.at[p], send_sem=ss, recv_sem=rs,
            device_id={"pts": (p + d) % PTSD}, device_id_type=MESH,
        )

    def start_scatter(src, dst, ss, rs):
        def step(d, carry):
            scatter_copy(d, src, dst, ss, rs).start()
            return carry

        lax.fori_loop(1, PTSD, step, 0)

    def start_gather(buf, ss, rs):
        def step(d, carry):
            gather_copy(d, buf, ss, rs).start()
            return carry

        lax.fori_loop(1, PTSD, step, 0)

    def wait_all(buf, sem):
        pltpu.make_async_copy(buf.at[pl.ds(0, PTSD - 1)], buf.at[pl.ds(0, PTSD - 1)], sem).wait()

    start_scatter(fbuf, frecv, rs_ss, rs_rs)
    for n in range(PLOC // 128):
        rows = pl.ds(n * 128, 128)
        jtre[rows, :] = jnp.transpose(jre[:, n * 128 : (n + 1) * 128].astype(F32))
        jtim[rows, :] = jnp.transpose(jim[:, n * 128 : (n + 1) * 128].astype(F32))
    wait_all(frecv, rs_rs)
    whole = fbuf[p]
    for d in range(PTSD - 1):
        whole = whole + frecv[d]
    agbuf[p] = whole
    start_gather(agbuf, ag_ss, ag_rs)
    wait_all(fbuf, rs_ss)
    wait_all(agbuf, ag_rs)

    for c in range(PTSD):
        covre[8 * c : 8 * c + 8, :] = agbuf[c, 0:8, :]
        covim[8 * c : 8 * c + 8, :] = agbuf[c, 8:16, :]
    for t in range(PTSD // 2):
        even = agbuf[2 * t, 16:24, :]
        odd = agbuf[2 * t + 1, 16:24, :]
        covre[256 + 8 * t : 264 + 8 * t, :] = jnp.where(low, even, pltpu.roll(odd, 4, 0))
        covim[256 + 8 * t : 264 + 8 * t, :] = jnp.where(low, pltpu.roll(even, 4, 0), odd)
    cre = covre[...]
    cim = covim[...]
    mrow = multb[...]
    neg = jnp.where(mrow > 0.0, -SHARPNESS * (cre * cre + cim * cim), NEG)
    peak = jnp.max(jnp.max(neg, axis=0, keepdims=True), axis=1, keepdims=True)
    expo = jnp.where(mrow > 0.0, jnp.exp(neg - peak), 0.0)
    part = jnp.sum(jnp.sum(mrow * expo, axis=0, keepdims=True), axis=1, keepdims=True)
    first = iota((8, BLOCK), 0) < 1
    stats[f] = jnp.where(first, jnp.broadcast_to(peak, (8, BLOCK)), jnp.broadcast_to(part, (8, BLOCK)))

    def feed_copies(buf, ss, rs):
        return [
            pltpu.make_async_remote_copy(
                src_ref=buf.at[f], dst_ref=buf.at[f], send_sem=ss.at[d - 1], recv_sem=rs.at[d - 1],
                device_id={"feed": (f + d) % FEED}, device_id_type=MESH,
            )
            for d in range(1, FEED)
        ]

    st_copies = feed_copies(stats, st_ss, st_rs)
    for c in st_copies:
        c.start()
    twice = 2.0 * expo
    st[0:128, :] = jnp.transpose(twice * cre)
    st[128:256, :] = jnp.transpose(twice * cim)

    def spread(s, carry):
        lanes = iota((1, CAP), 1).astype(F32)
        own = (lanes >= off_s[pl.ds(s, 1), 0:1]) & (lanes < end_s[pl.ds(s, 1), 0:1])
        part_s = jnp.where(own, st[...], 0.0).astype(BF16)
        grid = dot(part_s, ohm[...]).astype(BF16)
        gridf = grid.astype(F32)
        rate = jnp.concatenate([rates[s], rates[s]], axis=1)
        rr = (rate * gridf[0:128, :]).astype(BF16)
        ri = (rate * gridf[128:256, :]).astype(BF16)
        sr = grid[0:128, :]
        si = grid[128:256, :]
        top = pl.ds(pl.multiple_of(s * 256, 256), 128)
        bot = pl.ds(pl.multiple_of(s * 256 + 128, 128), 128)
        rhs[0, top, :] = sr
        rhs[1, top, :] = si
        rhs[2, top, :] = ri
        rhs[3, top, :] = -rr
        rhs[0, bot, :] = si
        rhs[1, bot, :] = -sr
        rhs[2, bot, :] = -rr
        rhs[3, bot, :] = -ri
        return carry

    lax.fori_loop(0, SLOTS, spread, 0)

    def backward(n, carry):
        accs[n] = dot(kall[...], rhs[n])
        return carry

    lax.fori_loop(0, 4, backward, 0)

    for c in st_copies:
        c.wait_recv()
    peaks = [stats[k, 0:1, 0:1] for k in range(FEED)]
    parts = [stats[k, 1:2, 0:1] for k in range(FEED)]
    top_peak = jnp.maximum(jnp.maximum(peaks[0], peaks[1]), jnp.maximum(peaks[2], peaks[3]))
    denom = sum(parts[k] * jnp.exp(peaks[k] - top_peak) for k in range(FEED))
    obj_ref[...] = -(top_peak + jnp.log(denom)) / SHARPNESS
    factor = scale * jnp.exp(peak - top_peak) / denom

    slope = factor * jnp.sum(jtre[...] * accs[2] + jtim[...] * accs[3], axis=1, keepdims=True)
    slope_row = jnp.transpose(jnp.broadcast_to(slope, (PLOC, 128)))[0:1, :]
    weighted = w16[...] * slope_row
    m = iota((32, 128), 0) * 128 + iota((32, 128), 1)
    grid_coef = jnp.zeros((32, 128), F32)
    for blk in range(PLOC // BLOCK):
        sums = jnp.sum(weighted[:, blk * BLOCK : (blk + 1) * BLOCK], axis=1, keepdims=True)
        i = m // NCV - row_ref[blk]
        j = m % NCV - col_ref[blk]
        key = jnp.where((i >= 0) & (i < 4) & (j >= 0) & (j < 4), 4 * i + j, -1)
        for k in range(16):
            grid_coef = grid_coef + jnp.where(key == k, sums[k : k + 1, :], 0.0)

    grad = jnp.concatenate([(factor * accs[0]).astype(BF16), (factor * accs[1]).astype(BF16)], axis=1)
    light = jnp.concatenate([il_all[k] for k in range(FEED)], axis=0)
    prod = dot(light, grad)
    pad_a[...] = jnp.full((8, BP), -1.0, F32)
    pad_a[0:1, 0:BEAMS] = bg_ref[...].astype(F32)
    grp = pad_a[0:1, :]
    ge_re = jnp.zeros((32, BP), F32)
    ge_im = jnp.zeros((32, BP), F32)
    for k in range(FEED):
        up = prod[128 * k : 128 * k + 64, :]
        dn = prod[128 * k + 64 : 128 * k + 128, :]
        re = up[:, 0:BP] + dn[:, BP:]
        im = up[:, BP:] - dn[:, 0:BP]
        for h in range(2):
            own = grp == float(2 * k + h)
            ge_re = ge_re + jnp.where(own, re[32 * h : 32 * h + 32, :], 0.0)
            ge_im = ge_im + jnp.where(own, im[32 * h : 32 * h + 32, :], 0.0)
    gbuf[...] = jnp.zeros((PTSD, 8, 128), F32)
    pieces = (ge_re[:, 0:128], ge_re[:, 128:], ge_im[:, 0:128], ge_im[:, 128:], grid_coef)
    for k, piece in enumerate(pieces):
        for c in range(PTSD):
            gbuf[c, k : k + 1, :] = piece[c : c + 1, :]

    start_scatter(gbuf, grecv, g_ss, g_rs)
    wait_all(grecv, g_rs)
    tile = gbuf[p]
    for d in range(PTSD - 1):
        tile = tile + grecv[d]
    fb[f] = tile
    fb_copies = feed_copies(fb, b_ss, b_rs)
    for c in fb_copies:
        c.start()
    for c in fb_copies:
        c.wait_recv()
    gag[p] = (fb[0] + fb[1]) + (fb[2] + fb[3])
    start_gather(gag, c_ss, c_rs)
    wait_all(gag, c_rs)

    for c in range(PTSD):
        gcoef_ref[c : c + 1, :] = gag[c, 4:5, :]
    half = [jnp.concatenate([gag[c, k : k + 1, :] for c in range(PTSD)], axis=0) for k in range(4)]
    for k in range(2):
        rows = jnp.concatenate([half[2 * k], half[2 * k + 1]], axis=1)
        pad_b[0:64, 0:128] = jnp.zeros((64, 128), F32)
        for b in range(2):
            lanes = slice(128 * b, 128 * b + 128)
            keep0 = grp[:, lanes] == (2 * f).astype(F32)
            keep1 = grp[:, lanes] == (2 * f + 1).astype(F32)
            pad_b[128 * b : 128 * b + 128, :] = jnp.zeros((128, 128), F32)
            pad_b[128 * b : 128 * b + GROUP_SIZE, :] = jnp.where(keep0, rows[0:GROUP_SIZE, lanes], 0.0)
            pad_b[128 * b + GROUP_SIZE : 128 * b + 2 * GROUP_SIZE, :] = jnp.where(
                keep1, rows[0:GROUP_SIZE, lanes], 0.0
            )
            out = jnp.transpose(pad_b[128 * b : 128 * b + 128, :])
            n = min(128, BEAMS - 128 * b)
            gexc_ref[k, 128 * b : 128 * b + n, :] = out[0:n, 0 : 2 * GROUP_SIZE]

    for c in il_copies + e_copies + st_copies + fb_copies:
        c.wait_send()
    wait_all(agbuf, ag_ss)
    wait_all(gbuf, g_ss)
    wait_all(gag, c_ss)


def local(
    illumination,
    excitation,
    beam_group,
    positions,
    params,
    span_rows,
    span_cols,
    surface_coef,
    directions,
    cover_blocks,
    cover_count,
):
    vmem = pl.BlockSpec(memory_space=pltpu.VMEM)
    smem = pl.BlockSpec(memory_space=pltpu.SMEM)
    dma = pltpu.SemaphoreType.DMA
    scratch = [
        pltpu.VMEM((FEED, 128, PLOC), BF16),
        pltpu.VMEM((FEED, EB, 128), BF16),
        pltpu.VMEM((NDB, BLOCK), F32),
        pltpu.VMEM((NDB, BLOCK), F32),
        pltpu.VMEM((PLOC, 128), F32),
        pltpu.VMEM((PLOC, 128), F32),
        pltpu.VMEM((PLOC, 128), F32),
        pltpu.VMEM((16, PLOC), F32),
        pltpu.VMEM((PLOC, SLOTS * 256), BF16),
        pltpu.VMEM((SLOTS, 128, 128), F32),
        pltpu.VMEM((8, BP), F32),
        pltpu.VMEM((BP, 128), F32),
        pltpu.VMEM((NDB, BP), F32),
        pltpu.VMEM((NDB, BP), F32),
        pltpu.VMEM((NDB, 128), F32),
        pltpu.VMEM((SLOTS, BP), F32),
        pltpu.VMEM((SLOTS, BP), F32),
        pltpu.VMEM((SLOTS, 128), F32),
        pltpu.VMEM((SLOTS, 128), F32),
        pltpu.VMEM((CAP, BP), BF16),
        pltpu.VMEM((CAP, BP), BF16),
        pltpu.VMEM((CAP, 128), F32),
        pltpu.VMEM((BP, PLOC), BF16),
        pltpu.VMEM((BP, PLOC), BF16),
        pltpu.VMEM((PLOC, BP), F32),
        pltpu.VMEM((PLOC, BP), F32),
        pltpu.VMEM((2 * CAP, PLOC), BF16),
        pltpu.VMEM((PTSD, CH, 128), F32),
        pltpu.VMEM((PTSD - 1, CH, 128), F32),
        pltpu.VMEM((PTSD, CH, 128), F32),
        pltpu.VMEM((CAP, 128), F32),
        pltpu.VMEM((CAP, 128), F32),
        pltpu.VMEM((256, CAP), F32),
        pltpu.VMEM((4, SLOTS * 256, BP), BF16),
        pltpu.VMEM((4, PLOC, BP), F32),
        pltpu.VMEM((FEED, 8, 128), F32),
        pltpu.VMEM((PTSD, 8, 128), F32),
        pltpu.VMEM((PTSD - 1, 8, 128), F32),
        pltpu.VMEM((FEED, 8, 128), F32),
        pltpu.VMEM((PTSD, 8, 128), F32),
        dma((3,)), dma((3,)), dma((3,)), dma((3,)),
        dma, dma, dma, dma,
        dma((3,)), dma((3,)),
        dma, dma,
        dma((3,)), dma((3,)),
        dma, dma,
    ]
    objective, grad_coef, grad_exc = pl.pallas_call(
        body,
        out_shape=(
            jax.ShapeDtypeStruct((1, 1), F32),
            jax.ShapeDtypeStruct((32, 128), F32),
            jax.ShapeDtypeStruct((2, BEAMS, 2 * GROUP_SIZE), F32),
        ),
        in_specs=[vmem, vmem, vmem, vmem, vmem, smem, smem, smem, vmem, vmem, vmem],
        out_specs=(vmem, vmem, vmem),
        scratch_shapes=scratch,
        compiler_params=pltpu.CompilerParams(
            collective_id=0, has_side_effects=True, vmem_limit_bytes=48 * 1024 * 1024
        ),
        name="coverage",
    )(
        illumination,
        excitation,
        beam_group.reshape(1, BEAMS),
        positions,
        params,
        span_rows,
        span_cols,
        surface_coef,
        directions,
        cover_blocks,
        cover_count.reshape(1, BEAMS),
    )
    return objective.reshape(()), grad_coef.reshape(NC), grad_exc


def solution(mesh):
    return jax.shard_map(
        local,
        mesh=mesh,
        in_specs=(
            P(None, "feed", "pts"),
            P(None, None, "feed"),
            P(),
            P(None, "pts"),
            P(None, "pts"),
            P("pts"),
            P("pts"),
            P(),
            P(),
            P(),
            P(),
        ),
        out_specs=(P(), P(), P(None, None, "feed")),
        check_vma=False,
    )
```

time: 1030 us -> 72.4 us (0.07)
  the two profiles are of different devices: /device:TPU:6 before, /device:TPU:1 now
where the time goes in v1:
time: 72.4 us; the launch traced here: 72.2 us
  Pallas kernels  66.4 us (92%)
  local copies, waits for them, and re-layouts  3.26 us (5%)
  between operations  2.54 us (4%)
    pallas_call x1, Pallas kernels, local(): pl.pallas_call(body, out_shape=(jax.ShapeDtypeStruct((1, 1), F32), jax.Sh...  66.4 us
    unnamed x25, local copies, waits for them, and re-layouts  3.26 us

profile of v1, /device:TPU:1, one launch (start us, length us, event | category | flops | bytes accessed | tf_op | source)
XLA Modules:
  0.0 72.2 jit_solution(12825290946666986327)
XLA Ops:
  0.6 0.0 copy-start.9
  0.6 0.0 copy-start.8
  0.6 1.0 %copy.15.ex_ref = bf16[2,200,50]{2,1,0:T(8,128)(2,1)S(1)} copy(bf16[2,200,50]{1,0,2:T(2,128)(2,1)} %param.12) | data formatting | bytes 80000 | tf_op args[1]
  1.6 0.0 copy-done.9
  1.6 0.1 copy.16.cb_ref
  1.8 0.0 copy-done.8
  1.8 0.0 copy-start
  1.8 0.0 copy-start.1
  1.8 0.0 copy-start.2
  1.8 0.0 copy-start.3
  1.8 0.0 copy-start.4
  1.8 0.0 copy-start.5
  1.8 0.0 copy-start.6
  1.8 0.0 copy-start.7
  1.9 0.7 %copy-done = f32[2,8192]{1,0:T(2,128)S(1)} copy-done((f32[2,8192]{1,0:T(2,128)S(1)}, f32[2,8192]{1,0:T(2,128)}, u32[]{:S(2)}) %copy-start) | copy-done | bytes 65560
  2.6 0.0 copy-done.1
  2.6 0.0 copy-done.2
  2.6 0.0 copy-done.3
  2.6 0.0 copy-done.4
  2.6 0.0 copy-done.5
  2.6 0.0 copy-done.6
  2.6 0.0 copy-done.7
  2.6 66.4 %coverage.1 = (f32[1,1]{1,0:T(1,128)}, f32[32,128]{1,0:T(8,128)S(1)}, f32[2,200,50]{2,1,0:T(8,128)S(1)}) custom-call(bf16[2,50,512]{2,1,0:T(8,128)(2,1)S(1)} %copy.14.il_ref, bf16[2,200,50]{2,1,0:T(8,128)(2,1)S(1)} %copy.15.ex_ref, s32[1,200]{1,0:T(1,128)S(1)} %bitcast.5, f32[2,512]{1,0:T(2,128)S(1)} %copy-done.2, f32[2,512]{1,0:T(2,128)S(1)} %copy-done.3, ...), custom_call_target="tpu_custom_call" | custom-call | tf_op jit(solution)/shard_map/coverage/pallas_call | solution.py:542
  69.0 0.8 %copy.17 = f32[2,200,50]{1,0,2:T(2,128)} copy(f32[2,200,50]{2,1,0:T(8,128)S(1)} %get-tuple-element.11) | data formatting | bytes 160000
  70.5 0.6 copy.21
  (1 shorter events, 0.0 us)
Async XLA Ops:
  0.6 1.0 %copy-start.9 = (s32[200,8]{0,1:T(8,128)S(1)}, s32[200,8]{0,1:T(8,128)}, u32[]{:S(2)}) copy-start(s32[200,8]{0,1:T(8,128)} %param.20) | copy-start | bytes 19204
  0.6 1.1 %copy-start.8 = (bf16[2,50,512]{2,0,1:T(2,128)(2,1)S(1)}, bf16[2,50,512]{2,0,1:T(2,128)(2,1)}, u32[]{:S(2)}) copy-start(bf16[2,50,512]{2,0,1:T(2,128)(2,1)} %param.11) | copy-start | bytes 307204
  1.8 0.8 %copy-start = (f32[2,8192]{1,0:T(2,128)S(1)}, f32[2,8192]{1,0:T(2,128)}, u32[]{:S(2)}) copy-start(f32[2,8192]{1,0:T(2,128)} %dir_ref.1) | copy-start | bytes 196612
  1.8 0.8 %copy-start.1 = (f32[4096]{0:T(1024)S(1)}, f32[4096]{0:T(1024)}, u32[]{:S(2)}) copy-start(f32[4096]{0:T(1024)} %coef_ref.1) | copy-start | bytes 49156
  1.8 0.8 %copy-start.2 = (f32[2,512]{1,0:T(2,128)S(1)}, f32[2,512]{1,0:T(2,128)}, u32[]{:S(2)}) copy-start(f32[2,512]{1,0:T(2,128)} %pos_ref.1) | copy-start | bytes 12292
  1.8 0.8 %copy-start.3 = (f32[2,512]{1,0:T(2,128)S(1)}, f32[2,512]{1,0:T(2,128)}, u32[]{:S(2)}) copy-start(f32[2,512]{1,0:T(2,128)} %par_ref.1) | copy-start | bytes 12292
  1.8 0.8 %copy-start.4 = (s32[200]{0:T(256)S(1)}, s32[200]{0:T(256)}, u32[]{:S(2)}) copy-start(s32[200]{0:T(256)} %param.13) | copy-start | bytes 2404
  1.8 0.8 %copy-start.5 = (s32[200]{0:T(256)S(1)}, s32[200]{0:T(256)}, u32[]{:S(2)}) copy-start(s32[200]{0:T(256)} %param.21) | copy-start | bytes 2404
  1.8 0.8 %copy-start.6 = (s32[4]{0:T(128)S(1)}, s32[4]{0:T(128)}, u32[]{:S(2)}) copy-start(s32[4]{0:T(128)} %row_ref.1) | copy-start | bytes 52
  1.8 0.8 %copy-start.7 = (s32[4]{0:T(128)S(1)}, s32[4]{0:T(128)}, u32[]{:S(2)}) copy-start(s32[4]{0:T(128)} %col_ref.1) | copy-start | bytes 52

commit v2 on v1

--- a/solution.py
+++ b/solution.py
@@ -31,6 +31,12 @@
 CAP = 384
 CH = 24
 NEG = -1e30
+PAIRS = 900
+WIDTH = tuple(-(-min(BEAMS, PAIRS // (FEED * s + 1)) // 16) * 16 for s in range(SLOTS))
+BASE = tuple(sum(WIDTH[:s]) for s in range(SLOTS))
+ROWS = -(-sum(WIDTH) // 128) * 128
+PLANE = 16
+RING = 8
 
 COS_C = (0.99999921, -19.73898036, 64.92865742, -85.27162153, 58.79049212, -21.07110563)
 SIN_C = (6.28318492, -41.34158923, 81.59994333, -76.61447253, 41.34288235, -12.47124354)
@@ -59,8 +65,8 @@
     il_ref, ex_ref, bg_ref, pos_ref, par_ref, row_ref, col_ref, coef_ref, dir_ref, cb_ref, cnt_ref,
     obj_ref, gcoef_ref, gexc_ref,
     il_all, e_all, dirx, diry, xb, yb, hb, w16, kall, rates, pad_a, pad_b,
-    rt_s, mt_s, rank_s, rs_s, ms_s, off_s, end_s, ohm, oh, multb, jre, jim, jtre, jtim, jsel,
-    fbuf, frecv, agbuf, covre, covim, st, rhs, accs, stats, gbuf, grecv, fb, gag,
+    rt_s, mt_s, rank_s, ohb, ohbt, ohc, ohct, multq, multb, jre, jim, jlre, jlim, fs,
+    fbuf, frecv, agbuf, covre, covim, sens, grid, yg, stats, gbuf, grecv, fb, gag, ring_sem, plane_sem,
     il_ss, il_rs, e_ss, e_rs, rs_ss, rs_rs, ag_ss, ag_rs, st_ss, st_rs, g_ss, g_rs, b_ss, b_rs, c_ss, c_rs,
 ):
     f = lax.axis_index("feed")
@@ -70,14 +76,19 @@
     par_sib = (sib + 2) % FEED
 
     barrier = pltpu.get_barrier_semaphore()
-
-    def greet(d, carry):
-        pl.semaphore_signal(barrier, inc=1, device_id={"pts": (p + d) % PTSD}, device_id_type=MESH)
-        return carry
-
-    lax.fori_loop(1, PTSD, greet, 0)
-    for d in range(1, FEED):
-        pl.semaphore_signal(barrier, inc=1, device_id={"feed": (f + d) % FEED}, device_id_type=MESH)
+    far = p // PLANE
+    flat = p % PLANE
+    y = p % 4
+    z = flat // 4
+    y_ring = [{"pts": p - y + (y + d) % 4} for d in range(1, 4)]
+    z_ring = [{"pts": p - 4 * z + 4 * ((z + d) % 4)} for d in range(1, 4)]
+    across = {"pts": (p + PLANE) % PTSD}
+    x_ring = [
+        {"feed": (f + d // 2) % FEED, "pts": (p + PLANE * (d % 2)) % PTSD} for d in range(1, RING)
+    ]
+    greeted = y_ring + z_ring + x_ring
+    for to in greeted:
+        pl.semaphore_signal(barrier, inc=1, device_id=to, device_id_type=MESH)
 
     r64 = iota((64, 50), 0)
     place = jnp.where(
@@ -101,7 +112,9 @@
     e_all[f, 0:BEAMS, :] = jnp.where(grp_cols == lane_grp, ex, 0.0).astype(BF16)
     e_all[f, BEAMS:EB, :] = jnp.zeros((EB - BEAMS, 128), BF16)
 
-    pl.semaphore_wait(barrier, PTSD - 1 + FEED - 1)
+    pl.semaphore_wait(barrier, len(greeted))
+    for to in y_ring:
+        pl.semaphore_signal(ring_sem, inc=1, device_id=to, device_id_type=MESH)
 
     def feed_copy(buf, slot, target, ss, rs, k):
         return pltpu.make_async_remote_copy(
@@ -149,9 +162,7 @@
     before = (bin_row == fq) & (lev_row < lev_b) & (lane < NDB)
     off_col = jnp.sum(jnp.where(before, n_row, 0.0), axis=1, keepdims=True)
     upper = jnp.where(iota((BP, BP), 0) < iota((BP, BP), 1), 1.0, 0.0).astype(BF16)
-    prefix = dot(ind.astype(BF16), upper)
-    mine = (ind > 0.0) & (bin_b[:, 0:1] == fq)
-    rt_s[...] = jnp.where(mine, prefix + off_col, -1.0)
+    rt_s[...] = jnp.where(ind > 0.0, dot(ind.astype(BF16), upper), -1.0)
     mt_s[...] = mult
     rank_s[...] = rank_b
     off_b = jnp.broadcast_to(off_col, (NDB, 128))
@@ -159,27 +170,29 @@
     def target(s):
         return 4 * s + f + (s % 2) * (3 - 2 * f)
 
+    used = BASE[-1] + WIDTH[-1]
+    ohb[used:ROWS, :] = jnp.zeros((ROWS - used, BP), BF16)
+    ohct[used:ROWS, :] = jnp.zeros((ROWS - used, CAP), BF16)
+    multq[used:ROWS, :] = jnp.zeros((ROWS - used, 128), F32)
     for s in range(SLOTS):
+        rows = slice(BASE[s], BASE[s] + WIDTH[s])
         is_s = rank_b == target(s).astype(F32)
-        off = jnp.sum(jnp.where(is_s, off_b, 0.0), axis=0, keepdims=True)
-        off_s[s : s + 1, :] = off
-        end_s[s : s + 1, :] = off + jnp.sum(jnp.where(is_s, n_b, 0.0), axis=0, keepdims=True)
+        off = jnp.sum(jnp.where(is_s, off_b, 0.0), axis=0, keepdims=True)[:, 0:1]
+        load = jnp.sum(jnp.where(is_s, n_b, 0.0), axis=0, keepdims=True)[:, 0:1]
         is_w = is_s[:, 0:1]
-        rs_s[s : s + 1, :] = jnp.sum(jnp.where(is_w, rt_s[...], 0.0), axis=0, keepdims=True)
-        ms_s[s : s + 1, :] = jnp.sum(jnp.where(is_w, mt_s[...], 0.0), axis=0, keepdims=True)
-
-    def one_hot(rc, carry):
-        base = pl.multiple_of(rc * 128, 128)
-        rows = (iota((128, BP), 0) + base).astype(F32)
-        acc = jnp.zeros((128, BP), F32)
-        for s in range(SLOTS):
-            acc = jnp.where(rs_s[s : s + 1, :] == rows, ms_s[s : s + 1, :], acc)
-        ohm[pl.ds(base, 128), :] = acc.astype(BF16)
-        oh[pl.ds(base, 128), :] = jnp.where(acc > 0.0, 1.0, 0.0).astype(BF16)
-        multb[pl.ds(base, 128), :] = jnp.broadcast_to(jnp.sum(acc, axis=1, keepdims=True), (128, 128))
-        return carry
-
-    lax.fori_loop(0, CAP // 128, one_hot, 0)
+        order = jnp.sum(jnp.where(is_w, rt_s[...], 0.0), axis=0, keepdims=True)
+        times = jnp.sum(jnp.where(is_w, mt_s[...], 0.0), axis=0, keepdims=True)
+        hit = order == iota((WIDTH[s], BP), 0).astype(F32)
+        ohb[rows, :] = jnp.where(hit, 1.0, 0.0).astype(BF16)
+        multq[rows, :] = jnp.broadcast_to(
+            jnp.sum(jnp.where(hit, times, 0.0), axis=1, keepdims=True), (WIDTH[s], 128)
+        )
+        w = iota((WIDTH[s], CAP), 0).astype(F32)
+        r = iota((WIDTH[s], CAP), 1).astype(F32)
+        ohct[rows, :] = jnp.where((r - w == off) & (w < load), 1.0, 0.0).astype(BF16)
+    for n in range(ROWS // 128):
+        cols = slice(128 * n, 128 * n + 128)
+        ohc[:, cols] = jnp.transpose(ohct[cols, :].astype(F32)).astype(BF16)
 
     def basis(t):
         m = 1.0 - t
@@ -219,7 +232,7 @@
         ux = jnp.sum(jnp.where(is_s, dirx[...], 0.0), axis=0, keepdims=True)
         uy = jnp.sum(jnp.where(is_s, diry[...], 0.0), axis=0, keepdims=True)
         uz1 = 1.0 + jnp.sqrt(1.0 - ux * ux - uy * uy)
-        rates[s] = columns(TWO_PI * uz1, 128)
+        rates[pl.ds(s, 1), :] = TWO_PI * uz1
         base = pl.multiple_of(s * 256, 256)
         for c in range(PLOC // 64):
             rows = pl.ds(64 * c, 64)
@@ -232,6 +245,9 @@
 
     lax.fori_loop(0, SLOTS, phases, 0)
 
+    pl.semaphore_wait(ring_sem, len(y_ring))
+    pl.semaphore_signal(plane_sem, inc=1, device_id=across, device_id_type=MESH)
+
     e_copies[0].wait_recv()
     e_copies.append(feed_copy(e_all, par, sib, e_ss, e_rs, 2))
     e_copies[2].start()
@@ -250,25 +266,24 @@
     jim[EB:BP, :] = jnp.zeros((BP - EB, PLOC), BF16)
     jre[0:EB, :] = dot(exc, mix_re).astype(BF16)
     jim[0:EB, :] = dot(exc, mix_im).astype(BF16)
-    jsel[0:CAP, :] = dot(oh[...], jre[...]).astype(BF16)
-    jsel[CAP : 2 * CAP, :] = dot(oh[...], jim[...]).astype(BF16)
-
-    covre[...] = jnp.zeros((CAP, BLOCK), F32)
-    covim[...] = jnp.zeros((CAP, BLOCK), F32)
+    jlre[...] = dot(ohb[...], jre[...]).astype(BF16)
+    jlim[...] = dot(ohb[...], jim[...]).astype(BF16)
     scale = 1.0 / math.sqrt(PLOC * PTSD)
 
-    def forward(s, carry):
-        base = pl.multiple_of(s * 256, 256)
-        prod = dot(jsel[...], kall[:, pl.ds(base, 256)])
-        row = iota((CAP, BLOCK), 0).astype(F32)
-        own = (row >= off_s[pl.ds(s, 1), :]) & (row < end_s[pl.ds(s, 1), :])
-        re = prod[0:CAP, 0:128] - prod[CAP:, 128:]
-        im = prod[0:CAP, 128:] + prod[CAP:, 0:128]
-        covre[...] = jnp.where(own, re, covre[...])
-        covim[...] = jnp.where(own, im, covim[...])
-        return carry
-
-    lax.fori_loop(0, SLOTS, forward, 0)
+    fs[used:ROWS, :] = jnp.zeros((ROWS - used, 512), BF16)
+    for s in range(SLOTS):
+        w = WIDTH[s]
+        rows = slice(BASE[s], BASE[s] + w)
+        prod = dot(jnp.concatenate([jlre[rows, :], jlim[rows, :]], axis=0), kall[:, 256 * s : 256 * s + 256])
+        re = prod[0:w, 0:128] - prod[w:, 128:]
+        im = prod[0:w, 128:] + prod[w:, 0:128]
+        for k, val in enumerate((re, im)):
+            high = val.astype(BF16)
+            fs[rows, 128 * k : 128 * k + 128] = high
+            fs[rows, 256 + 128 * k : 384 + 128 * k] = (val - high.astype(F32)).astype(BF16)
+    placed = dot(ohc[...], fs[...])
+    covre[...] = placed[:, 0:128] + placed[:, 256:384]
+    covim[...] = placed[:, 128:256] + placed[:, 384:512]
 
     low = iota((8, BLOCK), 0) < 4
     for c in range(PTSD):
@@ -310,11 +325,12 @@
     def wait_all(buf, sem):
         pltpu.make_async_copy(buf.at[pl.ds(0, PTSD - 1)], buf.at[pl.ds(0, PTSD - 1)], sem).wait()
 
+    pl.semaphore_wait(plane_sem, 1)
     start_scatter(fbuf, frecv, rs_ss, rs_rs)
-    for n in range(PLOC // 128):
-        rows = pl.ds(n * 128, 128)
-        jtre[rows, :] = jnp.transpose(jre[:, n * 128 : (n + 1) * 128].astype(F32))
-        jtim[rows, :] = jnp.transpose(jim[:, n * 128 : (n + 1) * 128].astype(F32))
+    for n in range(ROWS // 128):
+        cols = slice(128 * n, 128 * n + 128)
+        ohbt[:, cols] = jnp.transpose(ohb[cols, :].astype(F32)).astype(BF16)
+    multb[...] = dot(ohc[...], multq[...].astype(BF16))
     wait_all(frecv, rs_rs)
     whole = fbuf[p]
     for d in range(PTSD - 1):
@@ -355,39 +371,38 @@
     for c in st_copies:
         c.start()
     twice = 2.0 * expo
-    st[0:128, :] = jnp.transpose(twice * cre)
-    st[128:256, :] = jnp.transpose(twice * cim)
-
-    def spread(s, carry):
-        lanes = iota((1, CAP), 1).astype(F32)
-        own = (lanes >= off_s[pl.ds(s, 1), 0:1]) & (lanes < end_s[pl.ds(s, 1), 0:1])
-        part_s = jnp.where(own, st[...], 0.0).astype(BF16)
-        grid = dot(part_s, ohm[...]).astype(BF16)
-        gridf = grid.astype(F32)
-        rate = jnp.concatenate([rates[s], rates[s]], axis=1)
-        rr = (rate * gridf[0:128, :]).astype(BF16)
-        ri = (rate * gridf[128:256, :]).astype(BF16)
-        sr = grid[0:128, :]
-        si = grid[128:256, :]
-        top = pl.ds(pl.multiple_of(s * 256, 256), 128)
-        bot = pl.ds(pl.multiple_of(s * 256 + 128, 128), 128)
-        rhs[0, top, :] = sr
-        rhs[1, top, :] = si
-        rhs[2, top, :] = ri
-        rhs[3, top, :] = -rr
-        rhs[0, bot, :] = si
-        rhs[1, bot, :] = -sr
-        rhs[2, bot, :] = -rr
-        rhs[3, bot, :] = -ri
-        return carry
-
-    lax.fori_loop(0, SLOTS, spread, 0)
-
-    def backward(n, carry):
-        accs[n] = dot(kall[...], rhs[n])
-        return carry
-
-    lax.fori_loop(0, 4, backward, 0)
+    sens[:, 0:128] = (twice * cre).astype(BF16)
+    sens[:, 128:256] = (twice * cim).astype(BF16)
+    times = jnp.concatenate([multq[...], multq[...]], axis=1)
+    grid[...] = (times * dot(ohct[...], sens[...])).astype(BF16)
+
+    yg[used:ROWS, :] = jnp.zeros((ROWS - used, 2 * PLOC), BF16)
+    slope8 = jnp.zeros((8, PLOC), F32)
+    for s in range(SLOTS):
+        w = WIDTH[s]
+        rows = slice(BASE[s], BASE[s] + w)
+        sr = grid[rows, 0:128]
+        si = grid[rows, 128:256]
+        rate = rates[s : s + 1, :]
+        rr = (rate * sr.astype(F32)).astype(BF16)
+        ri = (rate * si.astype(F32)).astype(BF16)
+        left_s = jnp.concatenate(
+            [
+                jnp.concatenate([sr, si], axis=1),
+                jnp.concatenate([si, -sr], axis=1),
+                jnp.concatenate([ri, -rr], axis=1),
+                jnp.concatenate([-rr, -ri], axis=1),
+            ],
+            axis=0,
+        )
+        back = lax.dot_general(
+            left_s, kall[:, 256 * s : 256 * s + 256], (((1,), (1,)), ((), ())), preferred_element_type=F32
+        )
+        yg[rows, 0:PLOC] = back[0:w, :].astype(BF16)
+        yg[rows, PLOC:] = back[w : 2 * w, :].astype(BF16)
+        turn = jlre[rows, :].astype(F32) * back[2 * w : 3 * w, :] + jlim[rows, :].astype(F32) * back[3 * w :, :]
+        slope8 = slope8 + jnp.sum(turn.reshape(w // 8, 8, PLOC), axis=0)
+    slope_row = jnp.sum(slope8, axis=0, keepdims=True)
 
     for c in st_copies:
         c.wait_recv()
@@ -398,8 +413,6 @@
     obj_ref[...] = -(top_peak + jnp.log(denom)) / SHARPNESS
     factor = scale * jnp.exp(peak - top_peak) / denom
 
-    slope = factor * jnp.sum(jtre[...] * accs[2] + jtim[...] * accs[3], axis=1, keepdims=True)
-    slope_row = jnp.transpose(jnp.broadcast_to(slope, (PLOC, 128)))[0:1, :]
     weighted = w16[...] * slope_row
     m = iota((32, 128), 0) * 128 + iota((32, 128), 1)
     grid_coef = jnp.zeros((32, 128), F32)
@@ -411,9 +424,10 @@
         for k in range(16):
             grid_coef = grid_coef + jnp.where(key == k, sums[k : k + 1, :], 0.0)
 
-    grad = jnp.concatenate([(factor * accs[0]).astype(BF16), (factor * accs[1]).astype(BF16)], axis=1)
+    by_beam = dot(ohbt[...], yg[...]).astype(BF16)
+    grad = jnp.concatenate([by_beam[:, 0:PLOC], by_beam[:, PLOC:]], axis=0)
     light = jnp.concatenate([il_all[k] for k in range(FEED)], axis=0)
-    prod = dot(light, grad)
+    prod = lax.dot_general(light, grad, (((1,), (1,)), ((), ())), preferred_element_type=F32)
     pad_a[...] = jnp.full((8, BP), -1.0, F32)
     pad_a[0:1, 0:BEAMS] = bg_ref[...].astype(F32)
     grp = pad_a[0:1, :]
@@ -432,22 +446,51 @@
     pieces = (ge_re[:, 0:128], ge_re[:, 128:], ge_im[:, 0:128], ge_im[:, 128:], grid_coef)
     for k, piece in enumerate(pieces):
         for c in range(PTSD):
-            gbuf[c, k : k + 1, :] = piece[c : c + 1, :]
-
-    start_scatter(gbuf, grecv, g_ss, g_rs)
-    wait_all(grecv, g_rs)
-    tile = gbuf[p]
-    for d in range(PTSD - 1):
+            gbuf[c, k : k + 1, :] = factor * piece[c : c + 1, :]
+
+    def plane_scatter(d):
+        to = (flat + d) % PLANE
+        return pltpu.make_async_remote_copy(
+            src_ref=gbuf.at[pl.ds(2 * to, 2)], dst_ref=grecv.at[d - 1], send_sem=g_ss, recv_sem=g_rs,
+            device_id={"pts": p - flat + to}, device_id_type=MESH,
+        )
+
+    def plane_gather(d):
+        mine2 = gag.at[pl.ds(2 * flat, 2)]
+        return pltpu.make_async_remote_copy(
+            src_ref=mine2, dst_ref=mine2, send_sem=c_ss, recv_sem=c_rs,
+            device_id={"pts": p - flat + (flat + d) % PLANE}, device_id_type=MESH,
+        )
+
+    def wait_plane(sem):
+        pltpu.make_async_copy(grecv, grecv, sem).wait()
+
+    for d in range(1, PLANE):
+        plane_scatter(d).start()
+    wait_plane(g_rs)
+    tile = gbuf[pl.ds(2 * flat, 2)]
+    for d in range(PLANE - 1):
         tile = tile + grecv[d]
-    fb[f] = tile
-    fb_copies = feed_copies(fb, b_ss, b_rs)
+    spot = 2 * f + far
+    fb[spot] = tile
+    fb_copies = [
+        pltpu.make_async_remote_copy(
+            src_ref=fb.at[spot], dst_ref=fb.at[spot], send_sem=b_ss.at[k], recv_sem=b_rs.at[k],
+            device_id=to, device_id_type=MESH,
+        )
+        for k, to in enumerate(x_ring)
+    ]
     for c in fb_copies:
         c.start()
     for c in fb_copies:
         c.wait_recv()
-    gag[p] = (fb[0] + fb[1]) + (fb[2] + fb[3])
-    start_gather(gag, c_ss, c_rs)
-    wait_all(gag, c_rs)
+    total = fb[0]
+    for k in range(1, RING):
+        total = total + fb[k]
+    gag[pl.ds(2 * flat, 2)] = total
+    for d in range(1, PLANE):
+        plane_gather(d).start()
+    wait_plane(c_rs)
 
     for c in range(PTSD):
         gcoef_ref[c : c + 1, :] = gag[c, 4:5, :]
@@ -471,8 +514,8 @@
     for c in il_copies + e_copies + st_copies + fb_copies:
         c.wait_send()
     wait_all(agbuf, ag_ss)
-    wait_all(gbuf, g_ss)
-    wait_all(gag, c_ss)
+    wait_plane(g_ss)
+    wait_plane(c_ss)
 
 
 def local(
@@ -501,42 +544,43 @@
         pltpu.VMEM((PLOC, 128), F32),
         pltpu.VMEM((16, PLOC), F32),
         pltpu.VMEM((PLOC, SLOTS * 256), BF16),
-        pltpu.VMEM((SLOTS, 128, 128), F32),
+        pltpu.VMEM((SLOTS, 128), F32),
         pltpu.VMEM((8, BP), F32),
         pltpu.VMEM((BP, 128), F32),
         pltpu.VMEM((NDB, BP), F32),
         pltpu.VMEM((NDB, BP), F32),
         pltpu.VMEM((NDB, 128), F32),
-        pltpu.VMEM((SLOTS, BP), F32),
-        pltpu.VMEM((SLOTS, BP), F32),
-        pltpu.VMEM((SLOTS, 128), F32),
-        pltpu.VMEM((SLOTS, 128), F32),
-        pltpu.VMEM((CAP, BP), BF16),
-        pltpu.VMEM((CAP, BP), BF16),
+        pltpu.VMEM((ROWS, BP), BF16),
+        pltpu.VMEM((BP, ROWS), BF16),
+        pltpu.VMEM((CAP, ROWS), BF16),
+        pltpu.VMEM((ROWS, CAP), BF16),
+        pltpu.VMEM((ROWS, 128), F32),
         pltpu.VMEM((CAP, 128), F32),
         pltpu.VMEM((BP, PLOC), BF16),
         pltpu.VMEM((BP, PLOC), BF16),
-        pltpu.VMEM((PLOC, BP), F32),
-        pltpu.VMEM((PLOC, BP), F32),
-        pltpu.VMEM((2 * CAP, PLOC), BF16),
+        pltpu.VMEM((ROWS, PLOC), BF16),
+        pltpu.VMEM((ROWS, PLOC), BF16),
+        pltpu.VMEM((ROWS, 512), BF16),
         pltpu.VMEM((PTSD, CH, 128), F32),
         pltpu.VMEM((PTSD - 1, CH, 128), F32),
         pltpu.VMEM((PTSD, CH, 128), F32),
         pltpu.VMEM((CAP, 128), F32),
         pltpu.VMEM((CAP, 128), F32),
-        pltpu.VMEM((256, CAP), F32),
-        pltpu.VMEM((4, SLOTS * 256, BP), BF16),
-        pltpu.VMEM((4, PLOC, BP), F32),
+        pltpu.VMEM((CAP, 256), BF16),
+        pltpu.VMEM((ROWS, 256), BF16),
+        pltpu.VMEM((ROWS, 2 * PLOC), BF16),
         pltpu.VMEM((FEED, 8, 128), F32),
         pltpu.VMEM((PTSD, 8, 128), F32),
-        pltpu.VMEM((PTSD - 1, 8, 128), F32),
-        pltpu.VMEM((FEED, 8, 128), F32),
+        pltpu.VMEM((PLANE - 1, 2, 8, 128), F32),
+        pltpu.VMEM((RING, 2, 8, 128), F32),
         pltpu.VMEM((PTSD, 8, 128), F32),
+        pltpu.SemaphoreType.REGULAR,
+        pltpu.SemaphoreType.REGULAR,
         dma((3,)), dma((3,)), dma((3,)), dma((3,)),
         dma, dma, dma, dma,
         dma((3,)), dma((3,)),
         dma, dma,
-        dma((3,)), dma((3,)),
+        dma((RING - 1,)), dma((RING - 1,)),
         dma, dma,
     ]
     objective, grad_coef, grad_exc = pl.pallas_call(

time: 72.4 us -> 59.4 us (0.82)
  Pallas kernels: 66.4 us -> 53.4 us
    pallas_call x1, Pallas kernels: 66.4 us -> 53.4 us  [local(): pl.pallas_call(body, out_shape=(jax.ShapeDtypeStruct((1, 1), F32), jax.Sh...]
where the time goes in v2:
time: 59.4 us; the launch traced here: 59.2 us
  Pallas kernels  53.4 us (90%)
  local copies, waits for them, and re-layouts  3.26 us (5%)
  between operations  2.54 us (4%)
    pallas_call x1, Pallas kernels, local(): pl.pallas_call(body, out_shape=(jax.ShapeDtypeStruct((1, 1), F32), jax.Sh...  53.4 us
    unnamed x25, local copies, waits for them, and re-layouts  3.26 us

profile of v2, /device:TPU:1, one launch (start us, length us, event | category | flops | bytes accessed | tf_op | source)
XLA Modules:
  0.0 59.2 jit_solution(3986582606931641179)
XLA Ops:
  0.6 0.0 copy-start.9
  0.6 0.0 copy-start.8
  0.6 1.0 %copy.15.ex_ref = bf16[2,200,50]{2,1,0:T(8,128)(2,1)S(1)} copy(bf16[2,200,50]{1,0,2:T(2,128)(2,1)} %param.12) | data formatting | bytes 80000 | tf_op args[1]
  1.6 0.0 copy-done.9
  1.6 0.1 copy.16.cb_ref
  1.8 0.0 copy-done.8
  1.8 0.0 copy-start
  1.8 0.0 copy-start.1
  1.8 0.0 copy-start.2
  1.8 0.0 copy-start.3
  1.8 0.0 copy-start.4
  1.8 0.0 copy-start.5
  1.8 0.0 copy-start.6
  1.8 0.0 copy-start.7
  1.9 0.7 %copy-done = f32[2,8192]{1,0:T(2,128)S(1)} copy-done((f32[2,8192]{1,0:T(2,128)S(1)}, f32[2,8192]{1,0:T(2,128)}, u32[]{:S(2)}) %copy-start) | copy-done | bytes 65560
  2.6 0.0 copy-done.1
  2.6 0.0 copy-done.2
  2.6 0.0 copy-done.3
  2.6 0.0 copy-done.4
  2.6 0.0 copy-done.5
  2.6 0.0 copy-done.6
  2.6 0.0 copy-done.7
  2.6 53.4 %coverage.1 = (f32[1,1]{1,0:T(1,128)}, f32[32,128]{1,0:T(8,128)S(1)}, f32[2,200,50]{2,1,0:T(8,128)S(1)}) custom-call(bf16[2,50,512]{2,1,0:T(8,128)(2,1)S(1)} %copy.14.il_ref, bf16[2,200,50]{2,1,0:T(8,128)(2,1)S(1)} %copy.15.ex_ref, s32[1,200]{1,0:T(1,128)S(1)} %bitcast.5, f32[2,512]{1,0:T(2,128)S(1)} %copy-done.2, f32[2,512]{1,0:T(2,128)S(1)} %copy-done.3, ...), custom_call_target="tpu_custom_call" | custom-call | tf_op jit(solution)/shard_map/coverage/pallas_call | solution.py:586
  56.1 0.8 %copy.17 = f32[2,200,50]{1,0,2:T(2,128)} copy(f32[2,200,50]{2,1,0:T(8,128)S(1)} %get-tuple-element.11) | data formatting | bytes 160000
  57.5 0.6 %copy.21 = f32[4096]{0:T(1024)} copy(f32[4096]{0:T(1024)S(1)} %bitcast.4) | data formatting | bytes 32768
  (1 shorter events, 0.0 us)
Async XLA Ops:
  0.6 1.0 %copy-start.9 = (s32[200,8]{0,1:T(8,128)S(1)}, s32[200,8]{0,1:T(8,128)}, u32[]{:S(2)}) copy-start(s32[200,8]{0,1:T(8,128)} %param.20) | copy-start | bytes 19204
  0.6 1.1 %copy-start.8 = (bf16[2,50,512]{2,0,1:T(2,128)(2,1)S(1)}, bf16[2,50,512]{2,0,1:T(2,128)(2,1)}, u32[]{:S(2)}) copy-start(bf16[2,50,512]{2,0,1:T(2,128)(2,1)} %param.11) | copy-start | bytes 307204
  1.8 0.8 %copy-start = (f32[2,8192]{1,0:T(2,128)S(1)}, f32[2,8192]{1,0:T(2,128)}, u32[]{:S(2)}) copy-start(f32[2,8192]{1,0:T(2,128)} %dir_ref.1) | copy-start | bytes 196612
  1.8 0.8 %copy-start.1 = (f32[4096]{0:T(1024)S(1)}, f32[4096]{0:T(1024)}, u32[]{:S(2)}) copy-start(f32[4096]{0:T(1024)} %coef_ref.1) | copy-start | bytes 49156
  1.8 0.8 %copy-start.2 = (f32[2,512]{1,0:T(2,128)S(1)}, f32[2,512]{1,0:T(2,128)}, u32[]{:S(2)}) copy-start(f32[2,512]{1,0:T(2,128)} %pos_ref.1) | copy-start | bytes 12292
  1.8 0.8 %copy-start.3 = (f32[2,512]{1,0:T(2,128)S(1)}, f32[2,512]{1,0:T(2,128)}, u32[]{:S(2)}) copy-start(f32[2,512]{1,0:T(2,128)} %par_ref.1) | copy-start | bytes 12292
  1.8 0.8 %copy-start.4 = (s32[200]{0:T(256)S(1)}, s32[200]{0:T(256)}, u32[]{:S(2)}) copy-start(s32[200]{0:T(256)} %param.13) | copy-start | bytes 2404
  1.8 0.8 %copy-start.5 = (s32[200]{0:T(256)S(1)}, s32[200]{0:T(256)}, u32[]{:S(2)}) copy-start(s32[200]{0:T(256)} %param.21) | copy-start | bytes 2404
  1.8 0.8 %copy-start.6 = (s32[4]{0:T(128)S(1)}, s32[4]{0:T(128)}, u32[]{:S(2)}) copy-start(s32[4]{0:T(128)} %row_ref.1) | copy-start | bytes 52
  1.8 0.8 %copy-start.7 = (s32[4]{0:T(128)S(1)}, s32[4]{0:T(128)}, u32[]{:S(2)}) copy-start(s32[4]{0:T(128)} %col_ref.1) | copy-start | bytes 52

commit v3 on v2

--- a/solution.py
+++ b/solution.py
@@ -64,10 +64,10 @@
 def body(
     il_ref, ex_ref, bg_ref, pos_ref, par_ref, row_ref, col_ref, coef_ref, dir_ref, cb_ref, cnt_ref,
     obj_ref, gcoef_ref, gexc_ref,
-    il_all, e_all, dirx, diry, xb, yb, hb, w16, kall, rates, pad_a, pad_b,
+    il_all, e_all, dirx, diry, xb, yb, hb, w16, kall, rates, pad_a,
     rt_s, mt_s, rank_s, ohb, ohbt, ohc, ohct, multq, multb, jre, jim, jlre, jlim, fs,
-    fbuf, frecv, agbuf, covre, covim, sens, grid, yg, stats, gbuf, grecv, fb, gag, ring_sem, plane_sem,
-    il_ss, il_rs, e_ss, e_rs, rs_ss, rs_rs, ag_ss, ag_rs, st_ss, st_rs, g_ss, g_rs, b_ss, b_rs, c_ss, c_rs,
+    fbuf, frecv, agbuf, covre, covim, sens, grid, yg, stats, gbuf, grecv, fb, gag, next_sem, row_sem, plane_sem,
+    il_ss, il_rs, rs_ss, rs_rs, ag_ss, ag_rs, st_ss, st_rs, g_ss, g_rs, b_ss, b_rs, c_ss, c_rs,
 ):
     f = lax.axis_index("feed")
     p = lax.axis_index("pts")
@@ -81,12 +81,12 @@
     y = p % 4
     z = flat // 4
     y_ring = [{"pts": p - y + (y + d) % 4} for d in range(1, 4)]
-    z_ring = [{"pts": p - 4 * z + 4 * ((z + d) % 4)} for d in range(1, 4)]
+    z_next = [{"pts": p - 4 * z + 4 * ((z + d) % 4)} for d in (1, 3)]
     across = {"pts": (p + PLANE) % PTSD}
     x_ring = [
         {"feed": (f + d // 2) % FEED, "pts": (p + PLANE * (d % 2)) % PTSD} for d in range(1, RING)
     ]
-    greeted = y_ring + z_ring + x_ring
+    greeted = [{"feed": par}, {"feed": sib}, *y_ring, *z_next, across]
     for to in greeted:
         pl.semaphore_signal(barrier, inc=1, device_id=to, device_id_type=MESH)
 
@@ -94,8 +94,8 @@
     place = jnp.where(
         (iota((64, 50), 1) == GROUP_SIZE * (r64 // 32) + r64 % 32) & (r64 % 32 < GROUP_SIZE), 1.0, 0.0
     ).astype(BF16)
-    il_all[f, 0:64, :] = dot(place, il_ref[0]).astype(BF16)
-    il_all[f, 64:128, :] = dot(place, il_ref[1]).astype(BF16)
+    il_all[f, 0:64, :] = dot(place, il_ref[:, 0, :]).astype(BF16)
+    il_all[f, 64:128, :] = dot(place, il_ref[:, 1, :]).astype(BF16)
 
     pad_a[...] = jnp.full((8, BP), -1.0, F32)
     pad_a[0:1, 0:BEAMS] = bg_ref[...].astype(F32)
@@ -106,34 +106,19 @@
     fits = (r50 == lane_feed) & (l128 % 32 < GROUP_SIZE)
     q_re = jnp.where(fits & (l128 < 64), 1.0, 0.0).astype(BF16)
     q_im = jnp.where(fits & (l128 >= 64), 1.0, 0.0).astype(BF16)
-    ex = dot(ex_ref[0], q_re) + dot(ex_ref[1], q_im)
+    first_dims = (((0,), (0,)), ((), ()))
+    ex = lax.dot_general(ex_ref[:, 0, :], q_re, first_dims, preferred_element_type=F32)
+    ex = ex + lax.dot_general(ex_ref[:, 1, :], q_im, first_dims, preferred_element_type=F32)
     grp_cols = columns(grp_row, 128)[0:BEAMS, :]
     lane_grp = ((iota((BEAMS, 128), 1) % 64) // 32 + 2 * f).astype(F32)
     e_all[f, 0:BEAMS, :] = jnp.where(grp_cols == lane_grp, ex, 0.0).astype(BF16)
     e_all[f, BEAMS:EB, :] = jnp.zeros((EB - BEAMS, 128), BF16)
 
-    pl.semaphore_wait(barrier, len(greeted))
-    for to in y_ring:
-        pl.semaphore_signal(ring_sem, inc=1, device_id=to, device_id_type=MESH)
-
-    def feed_copy(buf, slot, target, ss, rs, k):
-        return pltpu.make_async_remote_copy(
-            src_ref=buf.at[slot], dst_ref=buf.at[slot], send_sem=ss.at[k], recv_sem=rs.at[k],
-            device_id={"feed": target}, device_id_type=MESH,
-        )
-
-    il_copies = [feed_copy(il_all, f, par, il_ss, il_rs, 0), feed_copy(il_all, f, sib, il_ss, il_rs, 1)]
-    e_copies = [feed_copy(e_all, f, par, e_ss, e_rs, 0), feed_copy(e_all, f, sib, e_ss, e_rs, 1)]
-    e_copies[0].start()
-    il_copies[0].start()
-    e_copies[1].start()
-    il_copies[1].start()
-
-    pad_b[...] = jnp.full((BP, 128), -1.0, F32)
-    pad_b[0:BEAMS, 0:CBMAX] = cb_ref[...].astype(F32)
+    pad_a[...] = jnp.full((8, BP), -1.0, F32)
+    pad_a[:, 0:BEAMS] = cb_ref[...].astype(F32)
+    cover = pad_a[...]
     pad_a[...] = jnp.zeros((8, BP), F32)
     pad_a[0:1, 0:BEAMS] = cnt_ref[...].astype(F32)
-    cover = jnp.transpose(pad_b[...])
     count = pad_a[0:1, :]
     k_io = iota((NDB, BP), 0).astype(F32)
     mult = jnp.zeros((NDB, BP), F32)
@@ -169,30 +154,6 @@
 
     def target(s):
         return 4 * s + f + (s % 2) * (3 - 2 * f)
-
-    used = BASE[-1] + WIDTH[-1]
-    ohb[used:ROWS, :] = jnp.zeros((ROWS - used, BP), BF16)
-    ohct[used:ROWS, :] = jnp.zeros((ROWS - used, CAP), BF16)
-    multq[used:ROWS, :] = jnp.zeros((ROWS - used, 128), F32)
-    for s in range(SLOTS):
-        rows = slice(BASE[s], BASE[s] + WIDTH[s])
-        is_s = rank_b == target(s).astype(F32)
-        off = jnp.sum(jnp.where(is_s, off_b, 0.0), axis=0, keepdims=True)[:, 0:1]
-        load = jnp.sum(jnp.where(is_s, n_b, 0.0), axis=0, keepdims=True)[:, 0:1]
-        is_w = is_s[:, 0:1]
-        order = jnp.sum(jnp.where(is_w, rt_s[...], 0.0), axis=0, keepdims=True)
-        times = jnp.sum(jnp.where(is_w, mt_s[...], 0.0), axis=0, keepdims=True)
-        hit = order == iota((WIDTH[s], BP), 0).astype(F32)
-        ohb[rows, :] = jnp.where(hit, 1.0, 0.0).astype(BF16)
-        multq[rows, :] = jnp.broadcast_to(
-            jnp.sum(jnp.where(hit, times, 0.0), axis=1, keepdims=True), (WIDTH[s], 128)
-        )
-        w = iota((WIDTH[s], CAP), 0).astype(F32)
-        r = iota((WIDTH[s], CAP), 1).astype(F32)
-        ohct[rows, :] = jnp.where((r - w == off) & (w < load), 1.0, 0.0).astype(BF16)
-    for n in range(ROWS // 128):
-        cols = slice(128 * n, 128 * n + 128)
-        ohc[:, cols] = jnp.transpose(ohct[cols, :].astype(F32)).astype(BF16)
 
     def basis(t):
         m = 1.0 - t
@@ -243,20 +204,62 @@
             kall[rows, pl.ds(base + 128, 128)] = (r * horner(SIN_C, z)).astype(BF16)
         return carry
 
-    lax.fori_loop(0, SLOTS, phases, 0)
-
-    pl.semaphore_wait(ring_sem, len(y_ring))
+    early = 3 * SLOTS // 4
+    lax.fori_loop(0, early, phases, 0)
+
+    pl.semaphore_wait(barrier, len(greeted))
+    for to in z_next:
+        pl.semaphore_signal(next_sem, inc=1, device_id=to, device_id_type=MESH)
+
+    def feed_copy(k, slot, to):
+        part = e_all.at[slot] if k % 3 == 0 else il_all.at[slot, pl.ds(64 * (k % 3 - 1), 64)]
+        return pltpu.make_async_remote_copy(
+            src_ref=part, dst_ref=part, send_sem=il_ss.at[k], recv_sem=il_rs.at[k],
+            device_id={"feed": to}, device_id_type=MESH,
+        )
+
+    to_par = [feed_copy(k, f, par) for k in range(3)]
+    to_sib = [feed_copy(k + 3, f, sib) for k in range(3)]
+    passed = [feed_copy(k + 6, par, sib) for k in range(3)]
+    for c in to_par + to_sib:
+        c.start()
+
+    lax.fori_loop(early, SLOTS, phases, 0)
+
+    used = BASE[-1] + WIDTH[-1]
+    ohb[used:ROWS, :] = jnp.zeros((ROWS - used, BP), BF16)
+    ohct[used:ROWS, :] = jnp.zeros((ROWS - used, CAP), BF16)
+    multq[used:ROWS, :] = jnp.zeros((ROWS - used, 128), F32)
+    for s in range(SLOTS):
+        rows = slice(BASE[s], BASE[s] + WIDTH[s])
+        is_s = rank_b == target(s).astype(F32)
+        off = jnp.sum(jnp.where(is_s, off_b, 0.0), axis=0, keepdims=True)[:, 0:1]
+        load = jnp.sum(jnp.where(is_s, n_b, 0.0), axis=0, keepdims=True)[:, 0:1]
+        is_w = is_s[:, 0:1]
+        order = jnp.sum(jnp.where(is_w, rt_s[...], 0.0), axis=0, keepdims=True)
+        times = jnp.sum(jnp.where(is_w, mt_s[...], 0.0), axis=0, keepdims=True)
+        hit = order == iota((WIDTH[s], BP), 0).astype(F32)
+        ohb[rows, :] = jnp.where(hit, 1.0, 0.0).astype(BF16)
+        multq[rows, :] = jnp.broadcast_to(
+            jnp.sum(jnp.where(hit, times, 0.0), axis=1, keepdims=True), (WIDTH[s], 128)
+        )
+        w = iota((WIDTH[s], CAP), 0).astype(F32)
+        r = iota((WIDTH[s], CAP), 1).astype(F32)
+        ohct[rows, :] = jnp.where((r - w == off) & (w < load), 1.0, 0.0).astype(BF16)
+    for n in range(ROWS // 128):
+        cols = slice(128 * n, 128 * n + 128)
+        ohc[:, cols] = jnp.transpose(ohct[cols, :].astype(F32)).astype(BF16)
+
+    pl.semaphore_wait(next_sem, len(z_next))
+    for to in z_next:
+        pl.semaphore_signal(row_sem, inc=1, device_id=to, device_id_type=MESH)
+    for c, onward in zip(to_par, passed):
+        c.wait_recv()
+        onward.start()
+    pl.semaphore_wait(row_sem, len(z_next))
     pl.semaphore_signal(plane_sem, inc=1, device_id=across, device_id_type=MESH)
-
-    e_copies[0].wait_recv()
-    e_copies.append(feed_copy(e_all, par, sib, e_ss, e_rs, 2))
-    e_copies[2].start()
-    il_copies[0].wait_recv()
-    il_copies.append(feed_copy(il_all, par, sib, il_ss, il_rs, 2))
-    il_copies[2].start()
-    for k in (1, 2):
-        e_copies[k].wait_recv()
-        il_copies[k].wait_recv()
+    for c in to_sib + passed:
+        c.wait_recv()
 
     exc = jnp.concatenate([e_all[k] for k in range(FEED)], axis=1)
     left = [il_all[k] for k in range(FEED)]
@@ -495,23 +498,14 @@
     for c in range(PTSD):
         gcoef_ref[c : c + 1, :] = gag[c, 4:5, :]
     half = [jnp.concatenate([gag[c, k : k + 1, :] for c in range(PTSD)], axis=0) for k in range(4)]
-    for k in range(2):
-        rows = jnp.concatenate([half[2 * k], half[2 * k + 1]], axis=1)
-        pad_b[0:64, 0:128] = jnp.zeros((64, 128), F32)
-        for b in range(2):
-            lanes = slice(128 * b, 128 * b + 128)
-            keep0 = grp[:, lanes] == (2 * f).astype(F32)
-            keep1 = grp[:, lanes] == (2 * f + 1).astype(F32)
-            pad_b[128 * b : 128 * b + 128, :] = jnp.zeros((128, 128), F32)
-            pad_b[128 * b : 128 * b + GROUP_SIZE, :] = jnp.where(keep0, rows[0:GROUP_SIZE, lanes], 0.0)
-            pad_b[128 * b + GROUP_SIZE : 128 * b + 2 * GROUP_SIZE, :] = jnp.where(
-                keep1, rows[0:GROUP_SIZE, lanes], 0.0
-            )
-            out = jnp.transpose(pad_b[128 * b : 128 * b + 128, :])
-            n = min(128, BEAMS - 128 * b)
-            gexc_ref[k, 128 * b : 128 * b + n, :] = out[0:n, 0 : 2 * GROUP_SIZE]
-
-    for c in il_copies + e_copies + st_copies + fb_copies:
+    for h in range(2):
+        keep = grp == (2 * f + h).astype(F32)
+        for k in range(2):
+            rows = jnp.concatenate([half[2 * k], half[2 * k + 1]], axis=1)
+            out = jnp.where(keep, rows, 0.0)
+            gexc_ref[GROUP_SIZE * h : GROUP_SIZE * (h + 1), k, :] = out[0:GROUP_SIZE, 0:BEAMS]
+
+    for c in to_par + to_sib + passed + st_copies + fb_copies:
         c.wait_send()
     wait_all(agbuf, ag_ss)
     wait_plane(g_ss)
@@ -546,7 +540,6 @@
         pltpu.VMEM((PLOC, SLOTS * 256), BF16),
         pltpu.VMEM((SLOTS, 128), F32),
         pltpu.VMEM((8, BP), F32),
-        pltpu.VMEM((BP, 128), F32),
         pltpu.VMEM((NDB, BP), F32),
         pltpu.VMEM((NDB, BP), F32),
         pltpu.VMEM((NDB, 128), F32),
@@ -576,7 +569,8 @@
         pltpu.VMEM((PTSD, 8, 128), F32),
         pltpu.SemaphoreType.REGULAR,
         pltpu.SemaphoreType.REGULAR,
-        dma((3,)), dma((3,)), dma((3,)), dma((3,)),
+        pltpu.SemaphoreType.REGULAR,
+        dma((9,)), dma((9,)),
         dma, dma, dma, dma,
         dma((3,)), dma((3,)),
         dma, dma,
@@ -588,7 +582,7 @@
         out_shape=(
             jax.ShapeDtypeStruct((1, 1), F32),
             jax.ShapeDtypeStruct((32, 128), F32),
-            jax.ShapeDtypeStruct((2, BEAMS, 2 * GROUP_SIZE), F32),
+            jax.ShapeDtypeStruct((2 * GROUP_SIZE, 2, BEAMS), F32),
         ),
         in_specs=[vmem, vmem, vmem, vmem, vmem, smem, smem, smem, vmem, vmem, vmem],
         out_specs=(vmem, vmem, vmem),
@@ -598,8 +592,8 @@
         ),
         name="coverage",
     )(
-        illumination,
-        excitation,
+        jnp.transpose(illumination, (1, 0, 2)),
+        jnp.transpose(excitation, (2, 0, 1)),
         beam_group.reshape(1, BEAMS),
         positions,
         params,
@@ -607,10 +601,10 @@
         span_cols,
         surface_coef,
         directions,
-        cover_blocks,
+        cover_blocks.T,
         cover_count.reshape(1, BEAMS),
     )
-    return objective.reshape(()), grad_coef.reshape(NC), grad_exc
+    return objective.reshape(()), grad_coef.reshape(NC), jnp.transpose(grad_exc, (1, 2, 0))
 
 
 def solution(mesh):

time: 59.4 us -> 66.6 us (1.12)
  local copies, waits for them, and re-layouts: 3.26 us -> 8.55 us
  Pallas kernels: 53.4 us -> 55.1 us
    unnamed x25 -> x24, local copies, waits for them, and re-layouts: 3.26 us -> 8.55 us
    pallas_call x1, Pallas kernels: 53.4 us -> 55.1 us  [local(): pl.pallas_call(body, out_shape=(jax.ShapeDtypeStruct((1, 1), F32), jax.Sh...]
where the time goes in v3:
time: 66.6 us; the launch traced here: 66.1 us
  Pallas kernels  55.1 us (83%)
  local copies, waits for them, and re-layouts  8.55 us (13%)
  between operations  2.42 us (4%)
    pallas_call x1, Pallas kernels, local(): pl.pallas_call(body, out_shape=(jax.ShapeDtypeStruct((1, 1), F32), jax.Sh...  55.1 us
    unnamed x24, local copies, waits for them, and re-layouts  8.55 us

profile of v3, /device:TPU:1, one launch (start us, length us, event | category | flops | bytes accessed | tf_op | source)
XLA Modules:
  0.0 66.1 jit_solution(15053990106723104331)
XLA Ops:
  0.6 0.0 copy-start.4
  0.6 0.0 copy-start.7
  0.7 0.7 %copy-done.4 = s32[200,8]{0,1:T(8,128)S(1)} copy-done((s32[200,8]{0,1:T(8,128)S(1)}, s32[200,8]{0,1:T(8,128)}, u32[]{:S(2)}) %copy-start.4) | copy-done | bytes 6424
  1.3 0.0 copy-done.7
  1.3 0.0 copy-start
  1.3 0.9 %copy-done = bf16[2,50,512]{2,0,1:T(2,128)(2,1)S(1)} copy-done((bf16[2,50,512]{2,0,1:T(2,128)(2,1)S(1)}, bf16[2,50,512]{2,0,1:T(2,128)(2,1)}, u32[]{:S(2)}) %copy-start) | copy-done | bytes 102424
  2.2 0.0 copy-start.1
  2.2 0.8 %copy-done.1 = f32[2,8192]{1,0:T(2,128)S(1)} copy-done((f32[2,8192]{1,0:T(2,128)S(1)}, f32[2,8192]{1,0:T(2,128)}, u32[]{:S(2)}) %copy-start.1) | copy-done | bytes 65560
  3.1 0.0 copy-start.2
  3.1 0.8 %copy-done.2 = bf16[2,200,50]{1,0,2:T(2,128)(2,1)S(1)} copy-done((bf16[2,200,50]{1,0,2:T(2,128)(2,1)S(1)}, bf16[2,200,50]{1,0,2:T(2,128)(2,1)}, u32[]{:S(2)}) %copy-start.2) | copy-done | bytes 40024
  3.9 0.0 copy-start.3
  3.9 0.7 %copy-done.3 = f32[4096]{0:T(1024)S(1)} copy-done((f32[4096]{0:T(1024)S(1)}, f32[4096]{0:T(1024)}, u32[]{:S(2)}) %copy-start.3) | copy-done | bytes 16408
  4.6 0.0 copy-start.5
  4.6 0.7 %copy-done.5 = f32[2,512]{1,0:T(2,128)S(1)} copy-done((f32[2,512]{1,0:T(2,128)S(1)}, f32[2,512]{1,0:T(2,128)}, u32[]{:S(2)}) %copy-start.5) | copy-done | bytes 4120
  5.3 0.0 copy-start.6
  5.3 0.7 %copy-done.6 = f32[2,512]{1,0:T(2,128)S(1)} copy-done((f32[2,512]{1,0:T(2,128)S(1)}, f32[2,512]{1,0:T(2,128)}, u32[]{:S(2)}) %copy-start.6) | copy-done | bytes 4120
  6.0 0.0 copy-start.8
  6.0 0.7 %copy-done.8 = s32[200]{0:T(256)S(1)} copy-done((s32[200]{0:T(256)S(1)}, s32[200]{0:T(256)}, u32[]{:S(2)}) %copy-start.8) | copy-done | bytes 824
  6.6 0.0 copy-start.9
  6.6 0.7 copy-done.9
  7.3 0.0 copy-start.10
  7.3 0.7 copy-done.10
  8.0 55.1 %coverage.1 = (f32[1,1]{1,0:T(1,128)}, f32[32,128]{1,0:T(8,128)S(1)}, f32[50,2,200]{2,1,0:T(2,128)S(1)}) custom-call(bf16[50,2,512]{2,1,0:T(2,128)(2,1)S(1)} %bitcast.9, bf16[50,2,200]{2,1,0:T(2,128)(2,1)S(1)} %bitcast.10, s32[1,200]{1,0:T(1,128)S(1)} %bitcast.13, f32[2,512]{1,0:T(2,128)S(1)} %copy-done.5, f32[2,512]{1,0:T(2,128)S(1)} %copy-done.6, ...), custom_call_target="tpu_custom_call" | custom-call | tf_op jit(solution)/shard_map/coverage/pallas_call | solution.py:580
  63.7 0.6 copy.18
  64.3 0.6 copy.19
Async XLA Ops:
  0.6 0.7 %copy-start.4 = (s32[200,8]{0,1:T(8,128)S(1)}, s32[200,8]{0,1:T(8,128)}, u32[]{:S(2)}) copy-start(s32[200,8]{0,1:T(8,128)} %param.20) | copy-start | bytes 19204
  0.6 0.7 %copy-start.7 = (s32[200]{0:T(256)S(1)}, s32[200]{0:T(256)}, u32[]{:S(2)}) copy-start(s32[200]{0:T(256)} %param.13) | copy-start | bytes 2404
  1.3 0.9 %copy-start = (bf16[2,50,512]{2,0,1:T(2,128)(2,1)S(1)}, bf16[2,50,512]{2,0,1:T(2,128)(2,1)}, u32[]{:S(2)}) copy-start(bf16[2,50,512]{2,0,1:T(2,128)(2,1)} %param.11) | copy-start | bytes 307204
  2.2 0.8 %copy-start.1 = (f32[2,8192]{1,0:T(2,128)S(1)}, f32[2,8192]{1,0:T(2,128)}, u32[]{:S(2)}) copy-start(f32[2,8192]{1,0:T(2,128)} %dir_ref.1) | copy-start | bytes 196612
  3.1 0.8 %copy-start.2 = (bf16[2,200,50]{1,0,2:T(2,128)(2,1)S(1)}, bf16[2,200,50]{1,0,2:T(2,128)(2,1)}, u32[]{:S(2)}) copy-start(bf16[2,200,50]{1,0,2:T(2,128)(2,1)} %param.12) | copy-start | bytes 120004
  3.9 0.7 %copy-start.3 = (f32[4096]{0:T(1024)S(1)}, f32[4096]{0:T(1024)}, u32[]{:S(2)}) copy-start(f32[4096]{0:T(1024)} %coef_ref.1) | copy-start | bytes 49156
  4.6 0.7 %copy-start.5 = (f32[2,512]{1,0:T(2,128)S(1)}, f32[2,512]{1,0:T(2,128)}, u32[]{:S(2)}) copy-start(f32[2,512]{1,0:T(2,128)} %pos_ref.1) | copy-start | bytes 12292
  5.3 0.7 %copy-start.6 = (f32[2,512]{1,0:T(2,128)S(1)}, f32[2,512]{1,0:T(2,128)}, u32[]{:S(2)}) copy-start(f32[2,512]{1,0:T(2,128)} %par_ref.1) | copy-start | bytes 12292
  6.0 0.7 %copy-start.8 = (s32[200]{0:T(256)S(1)}, s32[200]{0:T(256)}, u32[]{:S(2)}) copy-start(s32[200]{0:T(256)} %param.21) | copy-start | bytes 2404
  6.6 0.7 copy-start.9
  7.3 0.7 copy-start.10

commit v4 on v3

--- a/solution.py
+++ b/solution.py
@@ -62,8 +62,9 @@
 
 
 def body(
-    il_ref, ex_ref, bg_ref, pos_ref, par_ref, row_ref, col_ref, coef_ref, dir_ref, cb_ref, cnt_ref,
+    il_in, ex_in, bg_in, pos_in, par_in, row_in, col_in, coef_in, dir_in, cb_in, cnt_in,
     obj_ref, gcoef_ref, gexc_ref,
+    il_ref, ex_ref, bg_ref, pos_ref, par_ref, row_ref, col_ref, coef_ref, dir_ref, cb_ref, cnt_ref, in_sem,
     il_all, e_all, dirx, diry, xb, yb, hb, w16, kall, rates, pad_a,
     rt_s, mt_s, rank_s, ohb, ohbt, ohc, ohct, multq, multb, jre, jim, jlre, jlim, fs,
     fbuf, frecv, agbuf, covre, covim, sens, grid, yg, stats, gbuf, grecv, fb, gag, next_sem, row_sem, plane_sem,
@@ -89,6 +90,14 @@
     greeted = [{"feed": par}, {"feed": sib}, *y_ring, *z_next, across]
     for to in greeted:
         pl.semaphore_signal(barrier, inc=1, device_id=to, device_id_type=MESH)
+
+    held = (il_ref, ex_ref, bg_ref, cb_ref, cnt_ref, dir_ref, pos_ref, par_ref, coef_ref, row_ref, col_ref)
+    given = (il_in, ex_in, bg_in, cb_in, cnt_in, dir_in, pos_in, par_in, coef_in, row_in, col_in)
+    loads = [pltpu.make_async_copy(a, b, in_sem.at[k]) for k, (a, b) in enumerate(zip(given, held))]
+    for c in loads:
+        c.start()
+    for c in loads[:3]:
+        c.wait()
 
     r64 = iota((64, 50), 0)
     place = jnp.where(
@@ -113,6 +122,26 @@
     lane_grp = ((iota((BEAMS, 128), 1) % 64) // 32 + 2 * f).astype(F32)
     e_all[f, 0:BEAMS, :] = jnp.where(grp_cols == lane_grp, ex, 0.0).astype(BF16)
     e_all[f, BEAMS:EB, :] = jnp.zeros((EB - BEAMS, 128), BF16)
+
+    pl.semaphore_wait(barrier, len(greeted))
+    for to in z_next:
+        pl.semaphore_signal(next_sem, inc=1, device_id=to, device_id_type=MESH)
+
+    def feed_copy(k, slot, to):
+        part = e_all.at[slot] if k % 3 == 0 else il_all.at[slot, pl.ds(64 * (k % 3 - 1), 64)]
+        return pltpu.make_async_remote_copy(
+            src_ref=part, dst_ref=part, send_sem=il_ss.at[k], recv_sem=il_rs.at[k],
+            device_id={"feed": to}, device_id_type=MESH,
+        )
+
+    to_par = [feed_copy(k, f, par) for k in range(3)]
+    to_sib = [feed_copy(k + 3, f, sib) for k in range(3)]
+    passed = [feed_copy(k + 6, par, sib) for k in range(3)]
+    for c in to_par + to_sib:
+        c.start()
+
+    for c in loads[3:]:
+        c.wait()
 
     pad_a[...] = jnp.full((8, BP), -1.0, F32)
     pad_a[:, 0:BEAMS] = cb_ref[...].astype(F32)
@@ -204,27 +233,7 @@
             kall[rows, pl.ds(base + 128, 128)] = (r * horner(SIN_C, z)).astype(BF16)
         return carry
 
-    early = 3 * SLOTS // 4
-    lax.fori_loop(0, early, phases, 0)
-
-    pl.semaphore_wait(barrier, len(greeted))
-    for to in z_next:
-        pl.semaphore_signal(next_sem, inc=1, device_id=to, device_id_type=MESH)
-
-    def feed_copy(k, slot, to):
-        part = e_all.at[slot] if k % 3 == 0 else il_all.at[slot, pl.ds(64 * (k % 3 - 1), 64)]
-        return pltpu.make_async_remote_copy(
-            src_ref=part, dst_ref=part, send_sem=il_ss.at[k], recv_sem=il_rs.at[k],
-            device_id={"feed": to}, device_id_type=MESH,
-        )
-
-    to_par = [feed_copy(k, f, par) for k in range(3)]
-    to_sib = [feed_copy(k + 3, f, sib) for k in range(3)]
-    passed = [feed_copy(k + 6, par, sib) for k in range(3)]
-    for c in to_par + to_sib:
-        c.start()
-
-    lax.fori_loop(early, SLOTS, phases, 0)
+    lax.fori_loop(0, SLOTS, phases, 0)
 
     used = BASE[-1] + WIDTH[-1]
     ohb[used:ROWS, :] = jnp.zeros((ROWS - used, BP), BF16)
@@ -413,7 +422,7 @@
     parts = [stats[k, 1:2, 0:1] for k in range(FEED)]
     top_peak = jnp.maximum(jnp.maximum(peaks[0], peaks[1]), jnp.maximum(peaks[2], peaks[3]))
     denom = sum(parts[k] * jnp.exp(peaks[k] - top_peak) for k in range(FEED))
-    obj_ref[...] = -(top_peak + jnp.log(denom)) / SHARPNESS
+    obj_ref[...] = jnp.broadcast_to(-(top_peak + jnp.log(denom)) / SHARPNESS, (1, 128))
     factor = scale * jnp.exp(peak - top_peak) / denom
 
     weighted = w16[...] * slope_row
@@ -512,6 +521,17 @@
     wait_plane(c_ss)
 
 
+def store(obj_ref, gcoef_ref, gexc_ref, obj_out, gcoef_out, gexc_out, sem):
+    copies = [
+        pltpu.make_async_copy(a, b, sem.at[k])
+        for k, (a, b) in enumerate(((gexc_ref, gexc_out), (gcoef_ref, gcoef_out), (obj_ref, obj_out)))
+    ]
+    for c in copies:
+        c.start()
+    for c in copies:
+        c.wait()
+
+
 def local(
     illumination,
     excitation,
@@ -526,9 +546,25 @@
     cover_count,
 ):
     vmem = pl.BlockSpec(memory_space=pltpu.VMEM)
-    smem = pl.BlockSpec(memory_space=pltpu.SMEM)
+    hbm = pl.BlockSpec(memory_space=pltpu.HBM)
     dma = pltpu.SemaphoreType.DMA
+    values = (
+        jnp.transpose(illumination, (1, 0, 2)),
+        jnp.transpose(excitation, (2, 0, 1)),
+        beam_group.reshape(1, BEAMS),
+        positions,
+        params,
+        span_rows,
+        span_cols,
+        surface_coef,
+        directions,
+        cover_blocks.T,
+        cover_count.reshape(1, BEAMS),
+    )
+    scalar = (5, 6, 7)
     scratch = [
+        *[(pltpu.SMEM if k in scalar else pltpu.VMEM)(v.shape, v.dtype) for k, v in enumerate(values)],
+        dma((len(values),)),
         pltpu.VMEM((FEED, 128, PLOC), BF16),
         pltpu.VMEM((FEED, EB, 128), BF16),
         pltpu.VMEM((NDB, BLOCK), F32),
@@ -577,34 +613,31 @@
         dma((RING - 1,)), dma((RING - 1,)),
         dma, dma,
     ]
-    objective, grad_coef, grad_exc = pl.pallas_call(
+    shapes = (
+        jax.ShapeDtypeStruct((1, 128), F32),
+        jax.ShapeDtypeStruct((32, 128), F32),
+        jax.ShapeDtypeStruct((2 * GROUP_SIZE, 2, BEAMS), F32),
+    )
+    results = pl.pallas_call(
         body,
-        out_shape=(
-            jax.ShapeDtypeStruct((1, 1), F32),
-            jax.ShapeDtypeStruct((32, 128), F32),
-            jax.ShapeDtypeStruct((2 * GROUP_SIZE, 2, BEAMS), F32),
-        ),
-        in_specs=[vmem, vmem, vmem, vmem, vmem, smem, smem, smem, vmem, vmem, vmem],
+        out_shape=shapes,
+        in_specs=[hbm] * len(values),
         out_specs=(vmem, vmem, vmem),
         scratch_shapes=scratch,
         compiler_params=pltpu.CompilerParams(
-            collective_id=0, has_side_effects=True, vmem_limit_bytes=48 * 1024 * 1024
+            collective_id=0, has_side_effects=True, vmem_limit_bytes=60 * 1024 * 1024
         ),
         name="coverage",
-    )(
-        jnp.transpose(illumination, (1, 0, 2)),
-        jnp.transpose(excitation, (2, 0, 1)),
-        beam_group.reshape(1, BEAMS),
-        positions,
-        params,
-        span_rows,
-        span_cols,
-        surface_coef,
-        directions,
-        cover_blocks.T,
-        cover_count.reshape(1, BEAMS),
-    )
-    return objective.reshape(()), grad_coef.reshape(NC), jnp.transpose(grad_exc, (1, 2, 0))
+    )(*values)
+    objective, grad_coef, grad_exc = pl.pallas_call(
+        store,
+        out_shape=shapes,
+        in_specs=[vmem] * 3,
+        out_specs=(hbm, hbm, hbm),
+        scratch_shapes=[dma((3,))],
+        name="store",
+    )(*results)
+    return objective[0, 0], grad_coef.reshape(NC), jnp.transpose(grad_exc, (1, 2, 0))
 
 
 def solution(mesh):

time: 66.6 us -> 54.8 us (0.82)
  local copies, waits for them, and re-layouts: 8.55 us -> 0 us
  between operations: 2.42 us -> 0.64 us
  Pallas kernels: 55.1 us -> 54 us
    unnamed x24 -> x0, local copies, waits for them, and re-layouts: 8.55 us -> none
    pallas_call x1 -> x2, Pallas kernels: 55.1 us -> 54 us  [the longest x1 52.4 us: local(): pl.pallas_call(body, out_shape=shapes, in_specs=[hbm] * len(values), out_...]
where the time goes in v4:
time: 54.8 us; the launch traced here: 54.6 us
  Pallas kernels  54 us (99%)
  between operations  0.64 us (1%)
    pallas_call x1, Pallas kernels, local(): pl.pallas_call(body, out_shape=shapes, in_specs=[hbm] * len(values), out_...  52.4 us
    pallas_call x1, Pallas kernels, local(): pl.pallas_call(store, out_shape=shapes, in_specs=[vmem] * 3, out_specs=(h...  1.59 us

profile of v4, /device:TPU:1, one launch (start us, length us, event | category | flops | bytes accessed | tf_op | source)
XLA Modules:
  0.0 54.6 jit_solution(16484448904960027310)
XLA Ops:
  0.6 52.4 %coverage.1 = (f32[1,128]{1,0:T(1,128)}, f32[32,128]{1,0:T(8,128)}, f32[50,2,200]{2,1,0:T(2,128)}) custom-call(bf16[50,2,512]{2,1,0:T(2,128)(2,1)} %bitcast.9, bf16[50,2,200]{2,1,0:T(2,128)(2,1)} %bitcast.10, s32[1,200]{1,0:T(1,128)} %bitcast.12, f32[2,512]{1,0:T(2,128)} %pos_in.1, f32[2,512]{1,0:T(2,128)} %par_in.1, s32[4]{0:T(128)} %row_in.1, s32[4]{0:T(128)} %col_in.1, ...), custom_call_target="tpu_custom_call" | custom-call | tf_op jit(solution)/shard_map/coverage/pallas_call | solution.py:621
  53.0 1.6 %store.1 = (f32[1,128]{1,0:T(1,128)}, f32[32,128]{1,0:T(8,128)}, f32[50,2,200]{2,1,0:T(2,128)}) custom-call(f32[1,128]{1,0:T(1,128)} %get-tuple-element.9.obj_ref, f32[32,128]{1,0:T(8,128)} %get-tuple-element.10.gcoef_ref, f32[50,2,200]{2,1,0:T(2,128)} %get-tuple-element.11.gexc_ref), custom_call_target="tpu_custom_call" | custom-call | tf_op jit(solution)/shard_map/store/pallas_call | solution.py:632

commit v5 on v4

--- a/solution.py
+++ b/solution.py
@@ -67,7 +67,7 @@
     il_ref, ex_ref, bg_ref, pos_ref, par_ref, row_ref, col_ref, coef_ref, dir_ref, cb_ref, cnt_ref, in_sem,
     il_all, e_all, dirx, diry, xb, yb, hb, w16, kall, rates, pad_a,
     rt_s, mt_s, rank_s, ohb, ohbt, ohc, ohct, multq, multb, jre, jim, jlre, jlim, fs,
-    fbuf, frecv, agbuf, covre, covim, sens, grid, yg, stats, gbuf, grecv, fb, gag, next_sem, row_sem, plane_sem,
+    fbuf, frecv, agbuf, covre, covim, sens, peak_s, part_s, grid, yg, stats, gbuf, grecv, fb, gag, next_sem, row_sem, plane_sem,
     il_ss, il_rs, rs_ss, rs_rs, ag_ss, ag_rs, st_ss, st_rs, g_ss, g_rs, b_ss, b_rs, c_ss, c_rs,
 ):
     f = lax.axis_index("feed")
@@ -307,32 +307,30 @@
         fbuf[2 * t, 16:24, :] = jnp.where(low, re, pltpu.roll(im, 4, 0))
         fbuf[2 * t + 1, 16:24, :] = jnp.where(low, pltpu.roll(re, 4, 0), im)
 
-    def scatter_copy(d, src, dst, ss, rs):
-        to = (p + d) % PTSD
-        return pltpu.make_async_remote_copy(
-            src_ref=src.at[to], dst_ref=dst.at[d - 1], send_sem=ss, recv_sem=rs,
-            device_id={"pts": to}, device_id_type=MESH,
-        )
-
-    def gather_copy(d, buf, ss, rs):
-        return pltpu.make_async_remote_copy(
-            src_ref=buf.at[p], dst_ref=buf.at[p], send_sem=ss, recv_sem=rs,
-            device_id={"pts": (p + d) % PTSD}, device_id_type=MESH,
-        )
+    def hops(o):
+        return o[0] + min(o[1], 4 - o[1]) + min(o[2], 4 - o[2])
+
+    offsets = [(dx, dz, dy) for dx in range(2) for dz in range(4) for dy in range(4)][1:]
+    offsets.sort(key=hops, reverse=True)
+    near = [o for o in offsets if o[0] == 0]
+
+    def at_offset(o):
+        return PLANE * ((far + o[0]) % 2) + 4 * ((z + o[1]) % 4) + (y + o[2]) % 4
 
     def start_scatter(src, dst, ss, rs):
-        def step(d, carry):
-            scatter_copy(d, src, dst, ss, rs).start()
-            return carry
-
-        lax.fori_loop(1, PTSD, step, 0)
+        for k, o in enumerate(offsets):
+            to = at_offset(o)
+            pltpu.make_async_remote_copy(
+                src_ref=src.at[to], dst_ref=dst.at[k], send_sem=ss, recv_sem=rs,
+                device_id={"pts": to}, device_id_type=MESH,
+            ).start()
 
     def start_gather(buf, ss, rs):
-        def step(d, carry):
-            gather_copy(d, buf, ss, rs).start()
-            return carry
-
-        lax.fori_loop(1, PTSD, step, 0)
+        for o in offsets:
+            pltpu.make_async_remote_copy(
+                src_ref=buf.at[p], dst_ref=buf.at[p], send_sem=ss, recv_sem=rs,
+                device_id={"pts": at_offset(o)}, device_id_type=MESH,
+            ).start()
 
     def wait_all(buf, sem):
         pltpu.make_async_copy(buf.at[pl.ds(0, PTSD - 1)], buf.at[pl.ds(0, PTSD - 1)], sem).wait()
@@ -347,26 +345,45 @@
     whole = fbuf[p]
     for d in range(PTSD - 1):
         whole = whole + frecv[d]
-    agbuf[p] = whole
+
+    def total_of(x, op):
+        return op(op(x, axis=0, keepdims=True), axis=1, keepdims=True)
+
+    def thirds(x):
+        high = x.astype(BF16).astype(F32)
+        mid = (x - high).astype(BF16).astype(F32)
+        return [high, mid, x - high - mid]
+
+    re_a, im_a, both_b = whole[0:8], whole[8:16], whole[16:24]
+    times_a = multb[pl.ds(pl.multiple_of(8 * p, 8), 8), :]
+    times_b = multb[pl.ds(pl.multiple_of(256 + 8 * (p // 2), 8), 8), :]
+    turned = pltpu.roll(times_b, 4, 0)
+    times_b = jnp.where(low == (p % 2 == 0), times_b, turned)
+    square = both_b * both_b
+    neg_a = jnp.where(times_a > 0.0, -SHARPNESS * (re_a * re_a + im_a * im_a), NEG)
+    neg_b = jnp.where(times_b > 0.0, -SHARPNESS * (square + pltpu.roll(square, 4, 0)), NEG)
+    own_peak = total_of(jnp.maximum(neg_a, neg_b), jnp.max)
+    expo_a = jnp.where(times_a > 0.0, jnp.exp(neg_a - own_peak), 0.0)
+    expo_b = jnp.where(times_b > 0.0, jnp.exp(neg_b - own_peak), 0.0)
+    own_part = total_of(times_a * expo_a + jnp.where(low, times_b * expo_b, 0.0), jnp.sum)
+    notes = jnp.zeros((8, BLOCK), F32)
+    for k, val in enumerate(thirds(own_peak) + thirds(own_part)):
+        notes = jnp.where(iota((8, BLOCK), 0) == k, val, notes)
+    agbuf[p] = jnp.concatenate(
+        [2.0 * expo_a * re_a, 2.0 * expo_a * im_a, 2.0 * expo_b * both_b, notes], axis=0
+    ).astype(BF16)
     start_gather(agbuf, ag_ss, ag_rs)
     wait_all(fbuf, rs_ss)
     wait_all(agbuf, ag_rs)
 
     for c in range(PTSD):
-        covre[8 * c : 8 * c + 8, :] = agbuf[c, 0:8, :]
-        covim[8 * c : 8 * c + 8, :] = agbuf[c, 8:16, :]
-    for t in range(PTSD // 2):
-        even = agbuf[2 * t, 16:24, :]
-        odd = agbuf[2 * t + 1, 16:24, :]
-        covre[256 + 8 * t : 264 + 8 * t, :] = jnp.where(low, even, pltpu.roll(odd, 4, 0))
-        covim[256 + 8 * t : 264 + 8 * t, :] = jnp.where(low, pltpu.roll(even, 4, 0), odd)
-    cre = covre[...]
-    cim = covim[...]
-    mrow = multb[...]
-    neg = jnp.where(mrow > 0.0, -SHARPNESS * (cre * cre + cim * cim), NEG)
-    peak = jnp.max(jnp.max(neg, axis=0, keepdims=True), axis=1, keepdims=True)
-    expo = jnp.where(mrow > 0.0, jnp.exp(neg - peak), 0.0)
-    part = jnp.sum(jnp.sum(mrow * expo, axis=0, keepdims=True), axis=1, keepdims=True)
+        notes = agbuf[c, 16:32, :].astype(F32)[8:16]
+        peak_s[c : c + 1, :] = (notes[0:1] + notes[1:2]) + notes[2:3]
+        part_s[c : c + 1, :] = (notes[3:4] + notes[4:5]) + notes[5:6]
+    peak = jnp.max(peak_s[...], axis=0, keepdims=True)
+    gauge = jnp.exp(peak_s[...] - peak)
+    part = jnp.sum(part_s[...] * gauge, axis=0, keepdims=True)
+    peak_s[...] = gauge
     first = iota((8, BLOCK), 0) < 1
     stats[f] = jnp.where(first, jnp.broadcast_to(peak, (8, BLOCK)), jnp.broadcast_to(part, (8, BLOCK)))
 
@@ -382,11 +399,17 @@
     st_copies = feed_copies(stats, st_ss, st_rs)
     for c in st_copies:
         c.start()
-    twice = 2.0 * expo
-    sens[:, 0:128] = (twice * cre).astype(BF16)
-    sens[:, 128:256] = (twice * cim).astype(BF16)
+    for c in range(PTSD):
+        rows = agbuf[c, 0:16, :].astype(F32) * peak_s[c : c + 1, :]
+        sens[8 * c : 8 * c + 8, 0:128] = rows[0:8]
+        sens[8 * c : 8 * c + 8, 128:256] = rows[8:16]
+    for t in range(PTSD // 2):
+        even = agbuf[2 * t, 16:32, :].astype(F32)[0:8] * peak_s[2 * t : 2 * t + 1, :]
+        odd = agbuf[2 * t + 1, 16:32, :].astype(F32)[0:8] * peak_s[2 * t + 1 : 2 * t + 2, :]
+        sens[256 + 8 * t : 264 + 8 * t, 0:128] = jnp.where(low, even, pltpu.roll(odd, 4, 0))
+        sens[256 + 8 * t : 264 + 8 * t, 128:256] = jnp.where(low, pltpu.roll(even, 4, 0), odd)
     times = jnp.concatenate([multq[...], multq[...]], axis=1)
-    grid[...] = (times * dot(ohct[...], sens[...])).astype(BF16)
+    grid[...] = (times * dot(ohct[...], sens[...].astype(BF16))).astype(BF16)
 
     yg[used:ROWS, :] = jnp.zeros((ROWS - used, 2 * PLOC), BF16)
     slope8 = jnp.zeros((8, PLOC), F32)
@@ -423,7 +446,7 @@
     top_peak = jnp.maximum(jnp.maximum(peaks[0], peaks[1]), jnp.maximum(peaks[2], peaks[3]))
     denom = sum(parts[k] * jnp.exp(peaks[k] - top_peak) for k in range(FEED))
     obj_ref[...] = jnp.broadcast_to(-(top_peak + jnp.log(denom)) / SHARPNESS, (1, 128))
-    factor = scale * jnp.exp(peak - top_peak) / denom
+    factor = scale * jnp.exp(peak[:, 0:1] - top_peak) / denom
 
     weighted = w16[...] * slope_row
     m = iota((32, 128), 0) * 128 + iota((32, 128), 1)
@@ -460,25 +483,15 @@
         for c in range(PTSD):
             gbuf[c, k : k + 1, :] = factor * piece[c : c + 1, :]
 
-    def plane_scatter(d):
-        to = (flat + d) % PLANE
-        return pltpu.make_async_remote_copy(
-            src_ref=gbuf.at[pl.ds(2 * to, 2)], dst_ref=grecv.at[d - 1], send_sem=g_ss, recv_sem=g_rs,
-            device_id={"pts": p - flat + to}, device_id_type=MESH,
-        )
-
-    def plane_gather(d):
-        mine2 = gag.at[pl.ds(2 * flat, 2)]
-        return pltpu.make_async_remote_copy(
-            src_ref=mine2, dst_ref=mine2, send_sem=c_ss, recv_sem=c_rs,
-            device_id={"pts": p - flat + (flat + d) % PLANE}, device_id_type=MESH,
-        )
-
     def wait_plane(sem):
         pltpu.make_async_copy(grecv, grecv, sem).wait()
 
-    for d in range(1, PLANE):
-        plane_scatter(d).start()
+    for k, o in enumerate(near):
+        to = at_offset(o)
+        pltpu.make_async_remote_copy(
+            src_ref=gbuf.at[pl.ds(2 * (to % PLANE), 2)], dst_ref=grecv.at[k], send_sem=g_ss, recv_sem=g_rs,
+            device_id={"pts": to}, device_id_type=MESH,
+        ).start()
     wait_plane(g_rs)
     tile = gbuf[pl.ds(2 * flat, 2)]
     for d in range(PLANE - 1):
@@ -500,8 +513,12 @@
     for k in range(1, RING):
         total = total + fb[k]
     gag[pl.ds(2 * flat, 2)] = total
-    for d in range(1, PLANE):
-        plane_gather(d).start()
+    mine2 = gag.at[pl.ds(2 * flat, 2)]
+    for o in near:
+        pltpu.make_async_remote_copy(
+            src_ref=mine2, dst_ref=mine2, send_sem=c_ss, recv_sem=c_rs,
+            device_id={"pts": at_offset(o)}, device_id_type=MESH,
+        ).start()
     wait_plane(c_rs)
 
     for c in range(PTSD):
@@ -592,10 +609,12 @@
         pltpu.VMEM((ROWS, 512), BF16),
         pltpu.VMEM((PTSD, CH, 128), F32),
         pltpu.VMEM((PTSD - 1, CH, 128), F32),
-        pltpu.VMEM((PTSD, CH, 128), F32),
+        pltpu.VMEM((PTSD, 32, 128), BF16),
         pltpu.VMEM((CAP, 128), F32),
         pltpu.VMEM((CAP, 128), F32),
-        pltpu.VMEM((CAP, 256), BF16),
+        pltpu.VMEM((CAP, 256), F32),
+        pltpu.VMEM((PTSD, 128), F32),
+        pltpu.VMEM((PTSD, 128), F32),
         pltpu.VMEM((ROWS, 256), BF16),
         pltpu.VMEM((ROWS, 2 * PLOC), BF16),
         pltpu.VMEM((FEED, 8, 128), F32),

time: 54.8 us -> 52.3 us (0.954)
  Pallas kernels: 54 us -> 51.5 us
    pallas_call x1, Pallas kernels: 52.4 us -> 49.9 us  [local(): pl.pallas_call(body, out_shape=shapes, in_specs=[hbm] * len(values), out_...]
where the time goes in v5:
time: 52.3 us; the launch traced here: 52.2 us
  Pallas kernels  51.5 us (98%)
  between operations  0.64 us (1%)
    pallas_call x1, Pallas kernels, local(): pl.pallas_call(body, out_shape=shapes, in_specs=[hbm] * len(values), out_...  49.9 us
    pallas_call x1, Pallas kernels, local(): pl.pallas_call(store, out_shape=shapes, in_specs=[vmem] * 3, out_specs=(h...  1.59 us

profile of v5, /device:TPU:1, one launch (start us, length us, event | category | flops | bytes accessed | tf_op | source)
XLA Modules:
  0.0 52.2 jit_solution(13274474436889801058)
XLA Ops:
  0.6 49.9 %coverage.1 = (f32[1,128]{1,0:T(1,128)}, f32[32,128]{1,0:T(8,128)}, f32[50,2,200]{2,1,0:T(2,128)}) custom-call(bf16[50,2,512]{2,1,0:T(2,128)(2,1)} %bitcast.9, bf16[50,2,200]{2,1,0:T(2,128)(2,1)} %bitcast.10, s32[1,200]{1,0:T(1,128)} %bitcast.12, f32[2,512]{1,0:T(2,128)} %pos_in.1, f32[2,512]{1,0:T(2,128)} %par_in.1, s32[4]{0:T(128)} %row_in.1, s32[4]{0:T(128)} %col_in.1, ...), custom_call_target="tpu_custom_call" | custom-call | tf_op jit(solution)/shard_map/coverage/pallas_call | solution.py:640
  50.6 1.6 %store.1 = (f32[1,128]{1,0:T(1,128)}, f32[32,128]{1,0:T(8,128)}, f32[50,2,200]{2,1,0:T(2,128)}) custom-call(f32[1,128]{1,0:T(1,128)} %get-tuple-element.9.obj_ref, f32[32,128]{1,0:T(8,128)} %get-tuple-element.10.gcoef_ref, f32[50,2,200]{2,1,0:T(2,128)} %get-tuple-element.11.gexc_ref), custom_call_target="tpu_custom_call" | custom-call | tf_op jit(solution)/shard_map/store/pallas_call | solution.py:651

commit v6 on v5

--- a/solution.py
+++ b/solution.py
@@ -233,7 +233,13 @@
             kall[rows, pl.ds(base + 128, 128)] = (r * horner(SIN_C, z)).astype(BF16)
         return carry
 
-    lax.fori_loop(0, SLOTS, phases, 0)
+    lax.fori_loop(0, SLOTS // 2, phases, 0)
+    pl.semaphore_wait(next_sem, len(z_next))
+    for to in z_next:
+        pl.semaphore_signal(row_sem, inc=1, device_id=to, device_id_type=MESH)
+    lax.fori_loop(SLOTS // 2, SLOTS, phases, 0)
+    pl.semaphore_wait(row_sem, len(z_next))
+    pl.semaphore_signal(plane_sem, inc=1, device_id=across, device_id_type=MESH)
 
     used = BASE[-1] + WIDTH[-1]
     ohb[used:ROWS, :] = jnp.zeros((ROWS - used, BP), BF16)
@@ -259,14 +265,9 @@
         cols = slice(128 * n, 128 * n + 128)
         ohc[:, cols] = jnp.transpose(ohct[cols, :].astype(F32)).astype(BF16)
 
-    pl.semaphore_wait(next_sem, len(z_next))
-    for to in z_next:
-        pl.semaphore_signal(row_sem, inc=1, device_id=to, device_id_type=MESH)
     for c, onward in zip(to_par, passed):
         c.wait_recv()
         onward.start()
-    pl.semaphore_wait(row_sem, len(z_next))
-    pl.semaphore_signal(plane_sem, inc=1, device_id=across, device_id_type=MESH)
     for c in to_sib + passed:
         c.wait_recv()
 
@@ -439,15 +440,6 @@
         slope8 = slope8 + jnp.sum(turn.reshape(w // 8, 8, PLOC), axis=0)
     slope_row = jnp.sum(slope8, axis=0, keepdims=True)
 
-    for c in st_copies:
-        c.wait_recv()
-    peaks = [stats[k, 0:1, 0:1] for k in range(FEED)]
-    parts = [stats[k, 1:2, 0:1] for k in range(FEED)]
-    top_peak = jnp.maximum(jnp.maximum(peaks[0], peaks[1]), jnp.maximum(peaks[2], peaks[3]))
-    denom = sum(parts[k] * jnp.exp(peaks[k] - top_peak) for k in range(FEED))
-    obj_ref[...] = jnp.broadcast_to(-(top_peak + jnp.log(denom)) / SHARPNESS, (1, 128))
-    factor = scale * jnp.exp(peak[:, 0:1] - top_peak) / denom
-
     weighted = w16[...] * slope_row
     m = iota((32, 128), 0) * 128 + iota((32, 128), 1)
     grid_coef = jnp.zeros((32, 128), F32)
@@ -481,7 +473,7 @@
     pieces = (ge_re[:, 0:128], ge_re[:, 128:], ge_im[:, 0:128], ge_im[:, 128:], grid_coef)
     for k, piece in enumerate(pieces):
         for c in range(PTSD):
-            gbuf[c, k : k + 1, :] = factor * piece[c : c + 1, :]
+            gbuf[c, k : k + 1, :] = piece[c : c + 1, :]
 
     def wait_plane(sem):
         pltpu.make_async_copy(grecv, grecv, sem).wait()
@@ -496,8 +488,17 @@
     tile = gbuf[pl.ds(2 * flat, 2)]
     for d in range(PLANE - 1):
         tile = tile + grecv[d]
+
+    for c in st_copies:
+        c.wait_recv()
+    peaks = [stats[k, 0:1, 0:1] for k in range(FEED)]
+    parts = [stats[k, 1:2, 0:1] for k in range(FEED)]
+    top_peak = jnp.maximum(jnp.maximum(peaks[0], peaks[1]), jnp.maximum(peaks[2], peaks[3]))
+    denom = sum(parts[k] * jnp.exp(peaks[k] - top_peak) for k in range(FEED))
+    obj_ref[...] = jnp.broadcast_to(-(top_peak + jnp.log(denom)) / SHARPNESS, (1, 128))
+    factor = scale * jnp.exp(peak[:, 0:1] - top_peak) / denom
     spot = 2 * f + far
-    fb[spot] = tile
+    fb[spot] = tile * jnp.broadcast_to(factor, (8, BLOCK))
     fb_copies = [
         pltpu.make_async_remote_copy(
             src_ref=fb.at[spot], dst_ref=fb.at[spot], send_sem=b_ss.at[k], recv_sem=b_rs.at[k],

time: 52.3 us -> 50.9 us (0.973)
  Pallas kernels: 51.5 us -> 50.1 us
    pallas_call x1, Pallas kernels: 49.9 us -> 48.5 us  [local(): pl.pallas_call(body, out_shape=shapes, in_specs=[hbm] * len(values), out_...]
where the time goes in v6:
time: 50.9 us; the launch traced here: 50.8 us
  Pallas kernels  50.1 us (98%)
  between operations  0.64 us (1%)
    pallas_call x1, Pallas kernels, local(): pl.pallas_call(body, out_shape=shapes, in_specs=[hbm] * len(values), out_...  48.5 us
    pallas_call x1, Pallas kernels, local(): pl.pallas_call(store, out_shape=shapes, in_specs=[vmem] * 3, out_specs=(h...  1.59 us

profile of v6, /device:TPU:1, one launch (start us, length us, event | category | flops | bytes accessed | tf_op | source)
XLA Modules:
  0.0 50.8 jit_solution(3617245220217827363)
XLA Ops:
  0.6 48.5 %coverage.1 = (f32[1,128]{1,0:T(1,128)}, f32[32,128]{1,0:T(8,128)}, f32[50,2,200]{2,1,0:T(2,128)}) custom-call(bf16[50,2,512]{2,1,0:T(2,128)(2,1)} %bitcast.9, bf16[50,2,200]{2,1,0:T(2,128)(2,1)} %bitcast.10, s32[1,200]{1,0:T(1,128)} %bitcast.12, f32[2,512]{1,0:T(2,128)} %pos_in.1, f32[2,512]{1,0:T(2,128)} %par_in.1, s32[4]{0:T(128)} %row_in.1, s32[4]{0:T(128)} %col_in.1, ...), custom_call_target="tpu_custom_call" | custom-call | tf_op jit(solution)/shard_map/coverage/pallas_call | solution.py:641
  49.2 1.6 %store.1 = (f32[1,128]{1,0:T(1,128)}, f32[32,128]{1,0:T(8,128)}, f32[50,2,200]{2,1,0:T(2,128)}) custom-call(f32[1,128]{1,0:T(1,128)} %get-tuple-element.9.obj_ref, f32[32,128]{1,0:T(8,128)} %get-tuple-element.10.gcoef_ref, f32[50,2,200]{2,1,0:T(2,128)} %get-tuple-element.11.gexc_ref), custom_call_target="tpu_custom_call" | custom-call | tf_op jit(solution)/shard_map/store/pallas_call | solution.py:652

commit v7 on v6

--- a/solution.py
+++ b/solution.py
@@ -469,11 +469,26 @@
             own = grp == float(2 * k + h)
             ge_re = ge_re + jnp.where(own, re[32 * h : 32 * h + 32, :], 0.0)
             ge_im = ge_im + jnp.where(own, im[32 * h : 32 * h + 32, :], 0.0)
-    gbuf[...] = jnp.zeros((PTSD, 8, 128), F32)
-    pieces = (ge_re[:, 0:128], ge_re[:, 128:], ge_im[:, 0:128], ge_im[:, 128:], grid_coef)
-    for k, piece in enumerate(pieces):
-        for c in range(PTSD):
-            gbuf[c, k : k + 1, :] = piece[c : c + 1, :]
+
+    lane = iota((1, 128), 1)
+    free = 112
+
+    def start_lane(c, k):
+        return 64 * (k // 2) + 16 * (c // 4)
+
+    def spot_of(j, k):
+        return j // 2, slice(4 * (j % 2) + k, 4 * (j % 2) + k + 1)
+
+    last = grid_coef[24:32]
+    for k, piece in enumerate((ge_re[:, 0:128], ge_re[:, 128:], ge_im[:, 0:128], ge_im[:, 128:])):
+        for c in range(GROUP_SIZE):
+            row = piece[c : c + 1, :]
+            if k % 2 == 1 and c < 16:
+                turned = pltpu.roll(last, (free - start_lane(c, k)) % 128, 1)
+                row = jnp.where(lane >= free, turned[4 + c % 4 : 5 + c % 4, :], row)
+            gbuf[spot_of(c, k)] = row
+        for c in range(32 - GROUP_SIZE):
+            gbuf[spot_of(GROUP_SIZE + c, k)] = grid_coef[4 * c + k : 4 * c + k + 1, :]
 
     def wait_plane(sem):
         pltpu.make_async_copy(grecv, grecv, sem).wait()
@@ -481,11 +496,11 @@
     for k, o in enumerate(near):
         to = at_offset(o)
         pltpu.make_async_remote_copy(
-            src_ref=gbuf.at[pl.ds(2 * (to % PLANE), 2)], dst_ref=grecv.at[k], send_sem=g_ss, recv_sem=g_rs,
+            src_ref=gbuf.at[to % PLANE], dst_ref=grecv.at[k], send_sem=g_ss, recv_sem=g_rs,
             device_id={"pts": to}, device_id_type=MESH,
         ).start()
     wait_plane(g_rs)
-    tile = gbuf[pl.ds(2 * flat, 2)]
+    tile = gbuf[flat]
     for d in range(PLANE - 1):
         tile = tile + grecv[d]
 
@@ -513,24 +528,34 @@
     total = fb[0]
     for k in range(1, RING):
         total = total + fb[k]
-    gag[pl.ds(2 * flat, 2)] = total
-    mine2 = gag.at[pl.ds(2 * flat, 2)]
+    gag[flat] = total
+    mine = gag.at[flat]
     for o in near:
         pltpu.make_async_remote_copy(
-            src_ref=mine2, dst_ref=mine2, send_sem=c_ss, recv_sem=c_rs,
+            src_ref=mine, dst_ref=mine, send_sem=c_ss, recv_sem=c_rs,
             device_id={"pts": at_offset(o)}, device_id_type=MESH,
         ).start()
     wait_plane(c_rs)
 
-    for c in range(PTSD):
-        gcoef_ref[c : c + 1, :] = gag[c, 4:5, :]
-    half = [jnp.concatenate([gag[c, k : k + 1, :] for c in range(PTSD)], axis=0) for k in range(4)]
+    for k in range(4):
+        for c in range(32 - GROUP_SIZE):
+            gcoef_ref[4 * c + k : 4 * c + k + 1, :] = gag[spot_of(GROUP_SIZE + c, k)]
+    tails = [jnp.zeros((1, 128), F32)] * 4
+    for k in (1, 3):
+        for c in range(16):
+            begin = start_lane(c, k)
+            turned = pltpu.roll(gag[c // 2], (begin - free) % 128, 1)[spot_of(c, k)[1], :]
+            inside = (lane >= begin) & (lane < begin + 16)
+            tails[c % 4] = jnp.where(inside, turned, tails[c % 4])
+    for c in range(4):
+        gcoef_ref[28 + c : 29 + c, :] = tails[c]
+    half = [jnp.concatenate([gag[spot_of(c, k)] for c in range(GROUP_SIZE)], axis=0) for k in range(4)]
     for h in range(2):
         keep = grp == (2 * f + h).astype(F32)
         for k in range(2):
             rows = jnp.concatenate([half[2 * k], half[2 * k + 1]], axis=1)
             out = jnp.where(keep, rows, 0.0)
-            gexc_ref[GROUP_SIZE * h : GROUP_SIZE * (h + 1), k, :] = out[0:GROUP_SIZE, 0:BEAMS]
+            gexc_ref[GROUP_SIZE * h : GROUP_SIZE * (h + 1), k, :] = out[:, 0:BEAMS]
 
     for c in to_par + to_sib + passed + st_copies + fb_copies:
         c.wait_send()
@@ -619,10 +644,10 @@
         pltpu.VMEM((ROWS, 256), BF16),
         pltpu.VMEM((ROWS, 2 * PLOC), BF16),
         pltpu.VMEM((FEED, 8, 128), F32),
-        pltpu.VMEM((PTSD, 8, 128), F32),
-        pltpu.VMEM((PLANE - 1, 2, 8, 128), F32),
-        pltpu.VMEM((RING, 2, 8, 128), F32),
-        pltpu.VMEM((PTSD, 8, 128), F32),
+        pltpu.VMEM((PLANE, 8, 128), F32),
+        pltpu.VMEM((PLANE - 1, 8, 128), F32),
+        pltpu.VMEM((RING, 8, 128), F32),
+        pltpu.VMEM((PLANE, 8, 128), F32),
         pltpu.SemaphoreType.REGULAR,
         pltpu.SemaphoreType.REGULAR,
         pltpu.SemaphoreType.REGULAR,

time: 50.9 us -> 50.4 us (level)
    pallas_call x1, Pallas kernels: 48.5 us -> 48 us  [local(): pl.pallas_call(body, out_shape=shapes, in_specs=[hbm] * len(values), out_...]
where the time goes in v7:
time: 50.4 us; the launch traced here: 50.2 us
  Pallas kernels  49.6 us (98%)
  between operations  0.64 us (1%)
    pallas_call x1, Pallas kernels, local(): pl.pallas_call(body, out_shape=shapes, in_specs=[hbm] * len(values), out_...  48 us
    pallas_call x1, Pallas kernels, local(): pl.pallas_call(store, out_shape=shapes, in_specs=[vmem] * 3, out_specs=(h...  1.59 us

profile of v7, /device:TPU:1, one launch (start us, length us, event | category | flops | bytes accessed | tf_op | source)
XLA Modules:
  0.0 50.2 jit_solution(12486352310523963299)
XLA Ops:
  0.6 48.0 %coverage.1 = (f32[1,128]{1,0:T(1,128)}, f32[32,128]{1,0:T(8,128)}, f32[50,2,200]{2,1,0:T(2,128)}) custom-call(bf16[50,2,512]{2,1,0:T(2,128)(2,1)} %bitcast.9, bf16[50,2,200]{2,1,0:T(2,128)(2,1)} %bitcast.10, s32[1,200]{1,0:T(1,128)} %bitcast.12, f32[2,512]{1,0:T(2,128)} %pos_in.1, f32[2,512]{1,0:T(2,128)} %par_in.1, s32[4]{0:T(128)} %row_in.1, s32[4]{0:T(128)} %col_in.1, ...), custom_call_target="tpu_custom_call" | custom-call | tf_op jit(solution)/shard_map/coverage/pallas_call | solution.py:666
  48.6 1.6 %store.1 = (f32[1,128]{1,0:T(1,128)}, f32[32,128]{1,0:T(8,128)}, f32[50,2,200]{2,1,0:T(2,128)}) custom-call(f32[1,128]{1,0:T(1,128)} %get-tuple-element.9.obj_ref, f32[32,128]{1,0:T(8,128)} %get-tuple-element.10.gcoef_ref, f32[50,2,200]{2,1,0:T(2,128)} %get-tuple-element.11.gexc_ref), custom_call_target="tpu_custom_call" | custom-call | tf_op jit(solution)/shard_map/store/pallas_call | solution.py:677
